TPU v7x, 32 devices: a whole 2x2x4 slice. The times are simulated.
32 devices in a mesh: dp: 16 (over z, x, core), tensor: 2 (over y).
Axes of the slice: x: 2, y: 2, z: 4, core: 2. Of those that a mesh axis runs over, the one named last changes fastest.
Arguments:
- layer_input: bfloat16 [32768, 512], P(('dp', 'tensor')), may hold values from -6 to 6
- gene_known: int32 [32768], P('dp'), may hold values 0 or 1
- cell_genes: int32 [16, 4], P('dp'), may hold values from 0 to 2048, as said below
- w_qkv: bfloat16 [512, 3, 512], P(None, None, 'tensor'), may hold values from -0.25 to 0.25
- bias_qv: bfloat16 [2, 512], P(None, 'tensor'), may hold values from -3 to 3
- w_out: bfloat16 [512, 512], P('tensor'), may hold values from -4 to 4
- b_out: float32 [512], replicated, may hold values from -3 to 3
- ln1_gain: float32 [512], replicated, may hold values from 0.1 to 1.9
- ln1_bias: float32 [512], replicated, may hold values from -2 to 2
- w_up: bfloat16 [512, 512], P(None, 'tensor'), may hold values from -0.25 to 0.25
- b_up: bfloat16 [512], P('tensor'), may hold values from -3 to 3
- w_down: bfloat16 [512, 512], P('tensor'), may hold values from -0.25 to 0.25
- b_down: float32 [512], replicated, may hold values from -3 to 3
- ln2_gain: float32 [512], replicated, may hold values from 0.1 to 1.9
- ln2_bias: float32 [512], replicated, may hold values from -2 to 2
- cotangent: bfloat16 [32768, 512], P(('dp', 'tensor')), may hold values from -6 to 6
Outputs:
- activations: bfloat16 [32768, 512], P(('dp', 'tensor'))
- input_grad: float32 [32768, 512], P(('dp', 'tensor'))
- w_qkv_grad: float32 [512, 3, 512], P(None, None, 'tensor')
- bias_qv_grad: float32 [2, 512], P(None, 'tensor')
- w_out_grad: float32 [512, 512], P('tensor')
- b_out_grad: float32 [512], replicated
- ln1_gain_grad: float32 [512], replicated
- ln1_bias_grad: float32 [512], replicated
- w_up_grad: float32 [512, 512], P(None, 'tensor')
- b_up_grad: float32 [512], P('tensor')
- w_down_grad: float32 [512, 512], P('tensor')
- b_down_grad: float32 [512], replicated
- ln2_gain_grad: float32 [512], replicated
- ln2_bias_grad: float32 [512], replicated
Inputs may be any that keep to these rules, and one draw needn't show every extreme that they name: `cell_genes`: each row sums to 2048; a row is either 2048 followed by 4 - 1 zeros, or 4 positive lengths; at least one group holds a single cell.
All inputs are finite; a program needn't handle non-finite values. No bound on the sum of `gene_known` on one device may be relied on, other than what follows from the above.
Results may differ from a plain program's by a relative error of at most 0.019.
Values may be sent and summed in bfloat16 or wider, within the bound.
No kernel may reach another device: no remote copies, remote signals or barrier semaphores. Data moves between devices by JAX's collectives and lax.ppermute only.
A program may use at most 128 MiB of HBM per device.

v0:
```python
import functools

import jax
import jax.numpy as jnp
from jax import lax
from jax.experimental import pallas as pl
from jax.experimental.pallas import tpu as pltpu
from jax.sharding import PartitionSpec as P

HD = 64
LANES = 128
NORM_EPS = 1e-05
MASK_BIG = 2.0**100
LOG2E = 1.4426950408889634
VMEM_BYTES = 58 * 2**20
BF = jnp.bfloat16
F32 = jnp.float32
VMEM = pl.BlockSpec(memory_space=pltpu.VMEM)
HBM = pl.BlockSpec(memory_space=pl.ANY)


def dot(left, right, left_dim, right_dim):
    return lax.dot_general(
        left, right, (((left_dim,), (right_dim,)), ((), ())), preferred_element_type=F32
    )


def params():
    return pltpu.CompilerParams(vmem_limit_bytes=VMEM_BYTES)


def cost(macs, moved):
    return pl.CostEstimate(flops=2 * macs, bytes_accessed=moved, transcendentals=0)


def values_columns(rows):
    lane = lax.broadcasted_iota(jnp.int32, (rows, LANES), 1)
    return jnp.where((lane == HD) | (lane == HD + 1), 1.0, 0.0)


def live_rows(place_ref, first, rows, columns=slice(None)):
    place = place_ref[:, columns]
    row = lax.broadcasted_iota(jnp.int32, (rows, place.shape[1]), 0) + first
    return jnp.where(row == place, 1.0, 0.0).astype(BF)


def key_value_block(x_ref, place_ref, bounds_ref, w_refs, bias_ref, x_out, k_ref, v_ref, first, rows, base=0):
    at, to = pl.ds(first, rows), pl.ds(base + first, rows)
    later = slice(first, None) if isinstance(first, int) else slice(None)
    x = dot(live_rows(place_ref, first, rows, later), x_ref[later, :], 1, 0).astype(BF)
    x_out[at, :] = x
    shard = w_refs[0].shape[2]
    row = lax.broadcasted_iota(jnp.int32, (rows, LANES), 0) + first
    extra_k = jnp.where((row >= bounds_ref[0:1, :]) & (row < bounds_ref[1:2, :]), 1.0, 0.0)
    extra_v = values_columns(rows)
    low = lax.broadcasted_iota(jnp.int32, (rows, LANES), 1) < HD
    for side, w_ref in enumerate(w_refs):
        mine = slice(side * shard, (side + 1) * shard)
        keys = dot(x, w_ref[1], 1, 0)
        values = dot(x, w_ref[2], 1, 0) + bias_ref[1:2, mine]
        for i in range(shard // HD):
            pair = slice((i // 2) * LANES, (i // 2 + 1) * LANES)
            k_pair, v_pair = keys[:, pair], values[:, pair]
            if i % 2:
                k_pair, v_pair = pltpu.roll(k_pair, HD, 1), pltpu.roll(v_pair, HD, 1)
            h = side * (shard // HD) + i
            k_ref[h, to, :] = jnp.where(low, k_pair, extra_k).astype(BF)
            v_ref[h, to, :] = jnp.where(low, v_pair, extra_v).astype(BF)


def project_kernel(x_ref, own_ref, oth_ref, bias_ref, place_ref, bounds_ref, extra_q_ref, k_ref, v_ref, x_out, qt_ref, q_ref):
    block = q_ref.shape[0]
    first = pl.multiple_of(pl.program_id(0) * block, block)
    shard = own_ref.shape[2]
    key_value_block(
        x_ref, place_ref, bounds_ref, (own_ref, oth_ref), bias_ref, x_out, k_ref, v_ref, first, block
    )
    x = x_ref[pl.ds(first, block), :]
    for side, w_ref in enumerate((own_ref, oth_ref)):
        mine = slice(side * shard, (side + 1) * shard)
        q = (dot(x, w_ref[0], 1, 0) + bias_ref[0:1, mine]).astype(BF)
        q_ref[:, mine] = q
        turned = q.T
        for i in range(shard // HD):
            h = side * (shard // HD) + i
            qt_ref[h, :HD, :] = turned[i * HD : (i + 1) * HD, :]
            qt_ref[h, HD:, :] = extra_q_ref[...]


def project(x, w_own, w_oth, bias, place, bounds, extra_q):
    tokens, width = x.shape
    heads = width // HD
    block = 256
    whole = lambda *shape: pl.BlockSpec(shape, lambda i: (0,) * len(shape))
    per_head = whole(heads, tokens, LANES)
    return pl.pallas_call(
        project_kernel,
        grid=(tokens // block,),
        out_shape=(
            jax.ShapeDtypeStruct((heads, tokens, LANES), BF),
            jax.ShapeDtypeStruct((heads, tokens, LANES), BF),
            jax.ShapeDtypeStruct((tokens, width), BF),
            jax.ShapeDtypeStruct((heads, LANES, tokens), BF),
            jax.ShapeDtypeStruct((tokens, width), BF),
        ),
        in_specs=[
            whole(*x.shape),
            whole(*w_own.shape),
            whole(*w_oth.shape),
            whole(*bias.shape),
            whole(*place.shape),
            whole(*bounds.shape),
            pl.BlockSpec((HD, block), lambda i: (0, i)),
        ],
        out_specs=(
            per_head,
            per_head,
            whole(tokens, width),
            pl.BlockSpec((heads, LANES, block), lambda i: (0, 0, i)),
            pl.BlockSpec((block, width), lambda i: (i, 0)),
        ),
        compiler_params=params(),
        cost_estimate=cost(5 * tokens * width * width, 12 * tokens * width),
        name="project",
    )(x, w_own, w_oth, bias, place, bounds, extra_q)


def key_sizes(keys):
    return (keys * 13 // 16, keys)


def for_size(live, keys, work):
    below = 0
    for n, size in enumerate(key_sizes(keys)):

        @pl.when((live > below) & (live <= size) if below else live <= size)
        def _():
            work(size, n > 0)

        below = size


def sweep(rolled, size, count, body, carry=0):
    rows = size // count
    if rolled:
        return lax.fori_loop(0, count, lambda i, held: body(pl.multiple_of(i * rows, rows), held), carry)
    for i in range(count):
        carry = body(i * rows, carry)
    return carry


def attend_kernel(
    count, chunk, live_ref, qt_hbm, k_hbm, v_hbm, x_ref, own_ref, oth_ref, bias_ref, place_ref, bounds_ref,
    p_hbm, ot_ref, linv_ref, k_oth_hbm, v_oth_hbm, x_oth_hbm,
    qt_ref, k_ref, v_ref, x1_ref,
    s0_scr, s1_scr, peak0_scr, peak1_scr, row_scr, acc_scr, p_scr, sem, in_sem, out_sem,
):
    heads, _, queries = qt_ref.shape
    half = x_ref.shape[0]
    parts = queries // chunk
    steps = heads * parts
    slots = p_scr.shape[0]

    def copies_in(h):
        return [
            pltpu.make_async_copy(src.at[h], dst, in_sem.at[h, n])
            for n, (src, dst) in enumerate(
                ((qt_hbm, qt_ref.at[h]), (k_hbm, k_ref.at[h, :half]), (v_hbm, v_ref.at[h, :half]))
            )
        ]

    for h in range(heads):
        for copy in copies_in(h):
            copy.start()

    def project_live(size, rolled):
        def block(first, carry):
            key_value_block(
                x_ref, place_ref, bounds_ref, (own_ref, oth_ref), bias_ref, x1_ref, k_ref, v_ref, first, size // count, half
            )
            return carry

        sweep(rolled, size, count, block)
        if size < half:
            x1_ref[size:, :] = jnp.zeros((half - size, x1_ref.shape[1]), BF)

    for_size(live_ref[1], half, project_live)

    copies_kv = [
        pltpu.make_async_copy(k_ref.at[:, half:, :], k_oth_hbm, out_sem.at[0]),
        pltpu.make_async_copy(v_ref.at[:, half:, :], v_oth_hbm, out_sem.at[1]),
        pltpu.make_async_copy(x1_ref, x_oth_hbm, out_sem.at[2]),
    ]
    for copy in copies_kv:
        copy.start()

    def columns(step):
        return pl.ds(pl.multiple_of(lax.rem(step, parts) * chunk, chunk), chunk)

    def copies_out(step, size):
        slot = lax.rem(step, slots)
        copies = []
        for part in range(2):
            rows = slice(part * half, part * half + size)
            to = p_hbm.at[step // parts, rows, columns(step)]
            copies.append(pltpu.make_async_copy(p_scr.at[slot, rows, :], to, sem.at[slot, part]))
        return copies

    def scores(step, s_ref, peak, rows):
        s = dot(k_ref[step // parts, rows, :], qt_ref[step // parts, :, columns(step)], 1, 0)
        s_ref[rows, :] = s
        return jnp.maximum(peak, jnp.max(s.reshape(-1, 8, chunk), axis=0))

    def mix(step, s_ref, rows):
        p = jnp.exp2((s_ref[rows, :] - row_scr[...]) * (LOG2E * HD**-0.5)).astype(BF)
        p_scr[lax.rem(step, slots), rows, :] = p
        return dot(v_ref[step // parts, rows, :], p, 0, 0)

    def over_keys(size, rolled, block, carry):
        if size == half:
            return sweep(rolled, 2 * half, 2 * count, lambda at, held: block(pl.ds(at, size // count), held), carry)
        for part in range(2):
            rows = lambda at, held: block(pl.ds(part * half + at, size // count), held)
            carry = sweep(rolled, size, count, rows, carry)
        return carry

    def run(size, rolled, step, s_ref, peak_ref, after, s_after, peak_after):
        row_scr[...] = jnp.max(peak_ref[...], axis=0, keepdims=True)

        @pl.when(step >= slots)
        def _():
            for copy in copies_out(step - slots, size):
                copy.wait()

        def block(rows, held):
            peak = scores(after, s_after, held[0], rows)
            return peak, held[1] + mix(step, s_ref, rows)

        start = (jnp.full((8, chunk), -jnp.inf, F32), jnp.zeros((LANES, chunk), F32))
        peak_after[...], acc_scr[...] = over_keys(size, rolled, block, start)
        for copy in copies_out(step, size):
            copy.start()
        inverse = 1.0 / acc_scr[HD : HD + 1, :]
        linv_ref[step // parts, :, columns(step)] = inverse
        ot_ref[step // parts, :, columns(step)] = acc_scr[:HD, :] * inverse

    for copy in copies_in(0):
        copy.wait()

    def work(size, rolled):
        def first_block(rows, peak):
            return scores(0, s0_scr, peak, rows)

        peak0_scr[...] = over_keys(size, rolled, first_block, jnp.full((8, chunk), -jnp.inf, F32))

        @pl.loop(0, steps // 2)
        def _(i):
            run(size, rolled, 2 * i, s0_scr, peak0_scr, 2 * i + 1, s1_scr, peak1_scr)
            after = 2 * i + 2

            @pl.when((after < steps) & (lax.rem(after, parts) == 0))
            def _():
                for copy in copies_in(after // parts):
                    copy.wait()

            run(size, rolled, 2 * i + 1, s1_scr, peak1_scr, jnp.minimum(after, steps - 1), s0_scr, peak0_scr)

        for slot in range(slots):
            for copy in copies_out(steps - slots + slot, size):
                copy.wait()

    for_size(live_ref[1], half, work)
    for copy in copies_kv:
        copy.wait()


def attend(live, qt, k_own, v_own, x_oth, w_own, w_oth, bias, place, bounds):
    heads, _, queries = qt.shape
    keys = 2 * queries
    count, chunk, slots = 4, 512, 4
    per_head = jax.ShapeDtypeStruct(k_own.shape, BF)
    return pl.pallas_call(
        functools.partial(attend_kernel, count, chunk),
        out_shape=(
            jax.ShapeDtypeStruct((heads, keys, queries), BF),
            jax.ShapeDtypeStruct((heads, HD, queries), F32),
            jax.ShapeDtypeStruct((heads, 1, queries), F32),
            per_head,
            per_head,
            jax.ShapeDtypeStruct(x_oth.shape, BF),
        ),
        in_specs=[pl.BlockSpec(memory_space=pltpu.SMEM)] + [HBM] * 3 + [VMEM] * 6,
        out_specs=(HBM, VMEM, VMEM, HBM, HBM, HBM),
        scratch_shapes=[
            pltpu.VMEM(qt.shape, BF),
            pltpu.VMEM((heads, keys, LANES), BF),
            pltpu.VMEM((heads, keys, LANES), BF),
            pltpu.VMEM(x_oth.shape, BF),
            pltpu.VMEM((keys, chunk), F32),
            pltpu.VMEM((keys, chunk), F32),
            pltpu.VMEM((8, chunk), F32),
            pltpu.VMEM((8, chunk), F32),
            pltpu.VMEM((1, chunk), F32),
            pltpu.VMEM((LANES, chunk), F32),
            pltpu.VMEM((slots, keys, chunk), BF),
            pltpu.SemaphoreType.DMA((slots, 2)),
            pltpu.SemaphoreType.DMA((heads, 3)),
            pltpu.SemaphoreType.DMA((3,)),
        ],
        compiler_params=params(),
        cost_estimate=cost(heads * keys * queries * 512, 2 * heads * keys * queries),
        name="attend",
    )(live, qt, k_own, v_own, x_oth, w_own, w_oth, bias, place, bounds)


def normalize(values):
    mean = jnp.mean(values, axis=-1, keepdims=True)
    centered = values - mean
    inverse = lax.rsqrt(jnp.mean(centered * centered, axis=-1, keepdims=True) + NORM_EPS)
    return centered * inverse, inverse


def norm_back(e, normed, inverse):
    return inverse * (
        e - jnp.mean(e, axis=-1, keepdims=True) - normed * jnp.mean(e * normed, axis=-1, keepdims=True)
    )


def middle_kernel(
    sub, x_ref, cot_ref, ot_ref, linv_ref, w_own_ref, w_oth_ref, vec_ref,
    act_ref, res_ref, dot_ref, dnat_ref, own_ref, oth_ref, small_ref,
    att_scr, w_out_ref, w_up_ref, w_down_ref, b_up_ref, gw_ref,
):
    block, width = x_ref.shape
    heads = width // HD
    shard = width // 2
    b_out, gain1, bias1, b_down, gain2, bias2 = (vec_ref[i : i + 1, :] for i in range(6))

    @pl.when(pl.program_id(0) == 0)
    def _():
        gw_ref[...] = jnp.zeros_like(gw_ref)
        small_ref[...] = jnp.zeros_like(small_ref)
        for side, ref in enumerate((w_own_ref, w_oth_ref)):
            mine = slice(side * shard, (side + 1) * shard)
            w_out_ref[mine, :] = ref[:shard, :]
            w_down_ref[mine, :] = ref[shard : 2 * shard, :]
            w_up_ref[:shard, mine] = ref[2 * shard : 3 * shard, :shard]
            w_up_ref[shard:, mine] = ref[2 * shard : 3 * shard, shard:]
            b_up_ref[:, mine] = ref[3 * shard : 3 * shard + 1, :shard].astype(F32)

    def col_sum(row, values):
        small_ref[row : row + 1, :] += jnp.sum(values, axis=0, keepdims=True)

    def chain(u):
        rows = slice(u * sub, (u + 1) * sub)
        for h in range(heads):
            att_scr[u, h * HD : (h + 1) * HD, :] = ot_ref[h, :, rows].astype(BF)
        branch = dot(att_scr[u], w_out_ref[...], 0, 0)
        yield
        n1, inv1 = normalize(x_ref[rows, :].astype(F32) + branch + b_out)
        first = n1 * gain1 + bias1
        first_low = first.astype(BF)
        yield
        pre = dot(first_low, w_up_ref[...], 1, 0) + b_up_ref[...]
        yield
        cdf = 0.5 * (1.0 + lax.erf(pre * 0.5**0.5))
        hidden = (pre * cdf).astype(BF)
        slope = cdf + pre * (0.3989422804014327 * jnp.exp(-0.5 * pre * pre))
        yield
        branch = dot(hidden, w_down_ref[...], 1, 0)
        yield
        n2, inv2 = normalize(first + branch + b_down)
        act_ref[rows, :] = (n2 * gain2 + bias2).astype(BF)
        cot = cot_ref[rows, :].astype(F32)
        two = norm_back(cot * gain2, n2, inv2)
        two_low = two.astype(BF)
        yield
        back = dot(two_low, w_down_ref[...], 1, 1)
        gw_ref[2] += dot(hidden, two_low, 0, 0)
        col_sum(3, two)
        col_sum(4, cot * n2)
        col_sum(5, cot)
        yield
        pre_grad = (back * slope).astype(BF)
        yield
        back = dot(pre_grad, w_up_ref[...], 1, 1)
        gw_ref[1] += dot(first_low, pre_grad, 0, 0)
        col_sum(6, pre_grad.astype(F32))
        yield
        one = two + back
        res = norm_back(one * gain1, n1, inv1)
        res_ref[rows, :] = res
        res_low = res.astype(BF)
        yield
        turned = dot(w_out_ref[...], res_low, 1, 1)
        gw_ref[0] += dot(att_scr[u], res_low, 1, 0)
        col_sum(1, one * n1)
        col_sum(2, one)
        col_sum(0, res)
        yield
        pick = lax.broadcasted_iota(jnp.int32, (HD, sub), 0)
        for h in range(heads):
            head = slice(h * HD, (h + 1) * HD)
            grad = (turned[head].astype(BF).astype(F32) * linv_ref[h, :, rows]).astype(BF)
            inner = -jnp.sum(grad.astype(F32) * ot_ref[h, :, rows], axis=0, keepdims=True)
            high = inner.astype(BF).astype(F32)
            dot_ref[h, :HD, rows] = grad
            dot_ref[h, HD:, rows] = jnp.where(pick == 0, high, jnp.where(pick == 1, inner - high, 0.0)).astype(BF)
            att_scr[u, head, :] = grad
        dnat_ref[rows, :] = att_scr[u].T
        yield

    for _ in zip(*(chain(u) for u in range(block // sub))):
        pass

    @pl.when(pl.program_id(0) == pl.num_programs(0) - 1)
    def _():
        for ref, mine in ((own_ref, slice(0, shard)), (oth_ref, slice(shard, width))):
            ref[:shard, :] = gw_ref[0, mine, :].astype(ref.dtype)
            ref[shard:width, :] = gw_ref[2, mine, :].astype(ref.dtype)
            ref[width:, :shard] = gw_ref[1, :shard, mine].astype(ref.dtype)
            ref[width:, shard:] = gw_ref[1, shard:, mine].astype(ref.dtype)


def middle(x, cot, ot, linv, w_own, w_oth, vectors):
    tokens, width = x.shape
    heads = width // HD
    block, sub = 512, 256
    whole = lambda *shape: pl.BlockSpec(shape, lambda i: (0,) * len(shape))
    rows = pl.BlockSpec((block, width), lambda i: (i, 0))
    columns = lambda n: pl.BlockSpec((heads, n, block), lambda i: (0, 0, i))
    square = pltpu.VMEM((width, width), BF)
    return pl.pallas_call(
        functools.partial(middle_kernel, sub),
        grid=(tokens // block,),
        out_shape=(
            jax.ShapeDtypeStruct((tokens, width), BF),
            jax.ShapeDtypeStruct((tokens, width), F32),
            jax.ShapeDtypeStruct((heads, LANES, tokens), BF),
            jax.ShapeDtypeStruct((tokens, width), BF),
            jax.ShapeDtypeStruct((3 * width // 2, width), F32),
            jax.ShapeDtypeStruct((3 * width // 2, width), BF),
            jax.ShapeDtypeStruct((8, width), F32),
        ),
        in_specs=[rows, rows, columns(HD), columns(1), whole(*w_own.shape), whole(*w_oth.shape), whole(*vectors.shape)],
        out_specs=(
            rows, rows, columns(LANES), rows,
            whole(3 * width // 2, width), whole(3 * width // 2, width), whole(8, width),
        ),
        scratch_shapes=[
            pltpu.VMEM((block // sub, width, sub), BF), square, square, square,
            pltpu.VMEM((1, width), F32), pltpu.VMEM((3, width, width), F32),
        ],
        compiler_params=params(),
        cost_estimate=cost(9 * tokens * width * width, 20 * tokens * width),
        name="middle",
    )(x, cot, ot, linv, w_own, w_oth, vectors)


def times_weights(grad, own_ref, oth_ref, third):
    shard = own_ref.shape[2]
    return dot(grad[:, :shard], own_ref[third], 1, 1) + dot(grad[:, shard:], oth_ref[third], 1, 1)


def backward_kernel(sub, part, *refs):
    if part:
        (live_ref, place_ref, p_hbm, dot_hbm, dnat_hbm, q_hbm, k_hbm, v_hbm, x_hbm, own_hbm, oth_hbm,
         dq_hbm, dx_ref, gw_ref, bias_ref,
         dot_ref, dnat_ref, q_ref, k_ref, v_ref, x_ref, own_ref, oth_ref,
         dq_ref, dk_ref, dv_ref, dx_scr, acc_scr, p_scr, sem, pair_sem, last_sem, out_sem) = refs
        more = ((own_hbm, own_ref), (oth_hbm, oth_ref))
    else:
        (live_ref, small_ref, value_ref,
         p_hbm, dot_hbm, dnat_hbm, q_hbm, k_hbm, v_hbm, x_hbm, dq_hbm, gw_hbm, whole_hbm,
         sent_ref, kept_ref, dq_out, dk_hbm, dv_hbm,
         dot_ref, dnat_ref, q_ref, k_ref, v_ref, x_ref, before_ref, gw_ref, whole_ref,
         dq_ref, dk_ref, dv_ref, gq_ref, bias_ref, acc_scr, p_scr, sem, pair_sem, last_sem, out_sem) = refs
        more = ((dq_hbm, before_ref), (gw_hbm, gw_ref), (whole_hbm, whole_ref))
    heads, _, queries = dot_ref.shape
    keys = k_ref.shape[1]
    width = heads * HD
    shard = width // 2
    slots = p_scr.shape[0]
    pairs = heads // 2

    def copy_in(p, j, size):
        block = size // 2
        slot = lax.rem(p * 2 + j, slots)
        first = part * keys + j * block
        if not isinstance(j, int):
            first = pl.multiple_of(first, 16)
        src = p_hbm.at[pl.ds(2 * p, 2), pl.ds(first, block), :]
        return pltpu.make_async_copy(src, p_scr.at[slot, :, :block, :], sem.at[slot])

    def pair_copies(p):
        pair = pl.ds(2 * p, 2)
        lanes = pl.ds(pl.multiple_of(p * LANES, LANES), LANES)
        by_head = ((dot_hbm, dot_ref), (k_hbm, k_ref), (v_hbm, v_ref))
        by_lane = ((dnat_hbm, dnat_ref), (q_hbm, q_ref))
        return [
            pltpu.make_async_copy(src.at[pair], dst.at[pair], pair_sem.at[p, n]) for n, (src, dst) in enumerate(by_head)
        ] + [
            pltpu.make_async_copy(src.at[:, lanes], dst.at[:, lanes], pair_sem.at[p, 3 + n])
            for n, (src, dst) in enumerate(by_lane)
        ]

    last = ((x_hbm, x_ref),) + more

    def rows_out(p):
        rows = pl.ds(pl.multiple_of(p * 2 * HD, 2 * HD), 2 * HD)
        return pltpu.make_async_copy(dq_ref.at[rows, :], dq_hbm.at[rows, :], out_sem.at[p])

    last_copies = [pltpu.make_async_copy(src, dst, last_sem.at[n]) for n, (src, dst) in enumerate(last)]

    for copy in pair_copies(0):
        copy.start()

    def work(size, rolled):
        block, rows = size // 2, size // 4
        low = lax.broadcasted_iota(jnp.int32, (rows, LANES), 1) < HD
        if size < keys:
            dk_ref[size:, :] = jnp.zeros((keys - size, width), BF)
            dv_ref[size:, :] = jnp.zeros((keys - size, width), BF)
        for step in range(slots - 1):
            copy_in(step // 2, step % 2, size).start()

        @pl.loop(0, pairs)
        def _(p):
            lanes = pl.ds(pl.multiple_of(p * LANES, LANES), LANES)
            for copy in pair_copies(p):
                copy.wait()

            @pl.when(p + 1 < pairs)
            def _():
                for copy in pair_copies(p + 1):
                    copy.start()

            @pl.when(p == 1)
            def _():
                for copy in last_copies:
                    copy.start()

            acc_scr[...] = jnp.zeros_like(acc_scr)

            def one_block(j):
                slot = lax.rem(p * 2 + j, slots)
                copy_in(p, j, size).wait()
                ahead = 2 * p + j + slots - 1

                @pl.when(ahead < 2 * pairs)
                def _():
                    copy_in(ahead // 2, lax.rem(ahead, 2), size).start()

                def at_rows(at, total):
                    here = pl.ds(pl.multiple_of(j * block + at, 16), rows)
                    total, dks, dvs = list(total), [], []
                    for side in range(2):
                        h = 2 * p + side
                        prob = p_scr[slot, side, pl.ds(at, rows), :]
                        slope = dot(v_ref[h, here, :], dot_ref[h], 1, 0)
                        dvs.append(dot(prob, dnat_ref[:, lanes], 1, 0))
                        ds = (prob.astype(F32) * slope).astype(BF)
                        dks.append(dot(ds, q_ref[:, lanes], 1, 0))
                        total[side] = total[side] + dot(k_ref[h, here, :], ds, 0, 0)
                    dk_ref[here, lanes] = (jnp.where(low, dks[0], dks[1]) * HD**-0.5).astype(BF)
                    dv_ref[here, lanes] = jnp.where(low, dvs[0], dvs[1]).astype(BF)
                    return tuple(total)

                zero = jnp.zeros((LANES, queries), F32)
                for side, total in enumerate(sweep(rolled, block, 2, at_rows, (zero, zero))):
                    acc_scr[side] += total

            pl.loop(0, 2)(one_block)

            for side in range(2):
                dq_ref[pl.ds(pl.multiple_of((2 * p + side) * HD, HD), HD), :] = acc_scr[side, :HD, :]
            if part:
                rows_out(p).start()

    for_size(live_ref[1], keys, work)
    for copy in last_copies:
        copy.wait()
    bias_ref[...] = jnp.zeros_like(bias_ref)
    if part:
        gw_ref[...] = jnp.zeros_like(gw_ref)
        copies_out = [rows_out(p) for p in range(heads // 2)]
    else:
        gq_ref[...] = jnp.zeros_like(gq_ref)
        copies_out = [
            pltpu.make_async_copy(dk_ref, dk_hbm, out_sem.at[0]),
            pltpu.make_async_copy(dv_ref, dv_hbm, out_sem.at[1]),
        ]
        for copy in copies_out:
            copy.start()

    def weight_sums(size, rolled):
        def at_rows(at, carry):
            rows = pl.ds(at, size // 4)
            x, dk, dv = x_ref[rows, :], dk_ref[rows, :], dv_ref[rows, :]
            gw_ref[0] += dot(x, dk, 0, 0)
            gw_ref[1] += dot(x, dv, 0, 0)
            bias_ref[1:2, :] += jnp.sum(dv.astype(F32), axis=0, keepdims=True)
            if part:
                dx = times_weights(dk, own_ref, oth_ref, 1) + times_weights(dv, own_ref, oth_ref, 2)
                dx_scr[rows, :] = dx.astype(BF)
            return carry

        def back_in_place(at, carry):
            rows = pl.ds(at, sub)
            earlier = size if rolled else min(at + sub, size)
            dx_ref[rows, :] = dot(live_rows(place_ref, 0, earlier, rows), dx_scr[:earlier, :], 0, 0).astype(BF)
            return carry

        sweep(True, size, 4, at_rows)
        if part:
            sweep(rolled, keys, keys // sub, back_in_place)

    for_size(live_ref[1], keys, weight_sums)
    if not part:

        @pl.loop(0, queries // sub)
        def _(i):
            rows = pl.ds(pl.multiple_of(i * sub, sub), sub)
            dq = ((before_ref[:, rows] + dq_ref[:, rows]) * HD**-0.5).astype(BF).T
            dq_out[rows, :] = dq
            gq_ref[...] += dot(whole_ref[rows, :], dq, 0, 0)
            bias_ref[0:1, :] += jnp.sum(dq.astype(F32), axis=0, keepdims=True)

    if not part:
        first = live_ref[0] == 0
        bias_ref[1:2, :] += value_ref[1:2, :]
        cut = 3 * width // 2
        for side in range(2):
            mine = slice(side * shard, (side + 1) * shard)
            pieces = [gq_ref[:, mine], gw_ref[0, :, mine], gw_ref[1, :, mine]]
            blocks = [piece[at : at + shard, :].astype(BF) for piece in pieces for at in (0, shard)]
            for n in range(3):
                to = slice(side * cut + n * shard, side * cut + (n + 1) * shard)
                kept_ref[to, :] = jnp.where(first, blocks[n], blocks[3 + n])
                sent_ref[to, :] = jnp.where(first, blocks[3 + n], blocks[n])
            rows16 = [small_ref[:6, :shard], small_ref[6:7, mine], bias_ref[0:1, mine]]
            rows16 += [small_ref[:6, shard:], jnp.zeros((1, shard), F32), bias_ref[1:2, mine]]
            value = jnp.concatenate(rows16, axis=0)
            high = value.astype(BF)
            for n, half in enumerate((high, (value - high.astype(F32)).astype(BF))):
                to = slice(2 * cut + (2 * side + n) * 16, 2 * cut + (2 * side + n + 1) * 16)
                kept_ref[to, :] = half
                sent_ref[to, :] = half

    for copy in copies_out:
        copy.wait()


def attend_backward(part, first, probs, dot_turned, dnat, q, k, v, x, *more):
    heads, keys, queries = probs.shape
    width = heads * HD
    sub, slots = 256, 4
    sums = jax.ShapeDtypeStruct((2, width, width), F32)
    turned = jax.ShapeDtypeStruct((width, queries), F32)
    grad = jax.ShapeDtypeStruct((queries, width), BF)
    inputs = (dot_turned, dnat, q, k, v, x) + more
    held = [pltpu.VMEM(a.shape, a.dtype) for a in inputs]
    held += [pltpu.VMEM(turned.shape, F32), pltpu.VMEM(grad.shape, BF), pltpu.VMEM(grad.shape, BF)]
    if part:
        out_shape = (turned, grad, sums, jax.ShapeDtypeStruct((2, width), F32))
        out_specs = (HBM, VMEM, VMEM, VMEM)
        held.append(pltpu.VMEM(grad.shape, BF))
    else:
        payload = jax.ShapeDtypeStruct((3 * width + 64, width // 2), BF)
        out_shape = (payload, payload, grad, grad, grad)
        out_specs = (VMEM, VMEM, VMEM, HBM, HBM)
        held += [pltpu.VMEM((width, width), F32), pltpu.VMEM((2, width), F32)]
    first_specs = [pl.BlockSpec(memory_space=pltpu.SMEM), VMEM, VMEM][: len(first)]
    return pl.pallas_call(
        functools.partial(backward_kernel, sub, part),
        out_shape=out_shape,
        in_specs=first_specs + [HBM] * (1 + len(inputs)),
        out_specs=out_specs,
        scratch_shapes=held
        + [
            pltpu.VMEM((2, LANES, queries), F32),
            pltpu.VMEM((slots, 2, keys // 4, queries), BF),
            pltpu.SemaphoreType.DMA((slots,)),
            pltpu.SemaphoreType.DMA((heads // 2, 5)),
            pltpu.SemaphoreType.DMA((1 + len(more),)),
            pltpu.SemaphoreType.DMA((heads // 2,)),
        ],
        compiler_params=params(),
        cost_estimate=cost(heads * keys * queries * 512, heads * keys * queries),
        name="attend_back_own" if not part else "attend_back_other",
    )(*first, probs, *inputs)


def input_kernel(res_ref, got_ref, dq_ref, dk_ref, dv_ref, own_ref, oth_ref, place_ref, dx_ref, live_scr):
    @pl.when(pl.program_id(0) == 0)
    def _():
        @pl.loop(0, live_scr.shape[0] // 256)
        def _(i):
            rows = pl.ds(pl.multiple_of(i * 256, 256), 256)
            live_scr[rows, :] = (
                times_weights(dk_ref[rows, :], own_ref, oth_ref, 1) + times_weights(dv_ref[rows, :], own_ref, oth_ref, 2)
            ).astype(BF)

    dx = res_ref[...] + got_ref[...].astype(F32) + times_weights(dq_ref[...], own_ref, oth_ref, 0)
    dx_ref[...] = dx + dot(live_rows(place_ref, 0, live_scr.shape[0]), live_scr[...], 0, 0)


def input_gradient(res, got, dq, dk, dv, w_own, w_oth, place):
    tokens, width = res.shape
    rows = pl.BlockSpec((256, width), lambda i: (i, 0))
    whole = lambda *shape: pl.BlockSpec(shape, lambda i: (0,) * len(shape))
    return pl.pallas_call(
        input_kernel,
        grid=(tokens // 256,),
        out_shape=jax.ShapeDtypeStruct((tokens, width), F32),
        in_specs=[rows] * 3 + [whole(*dk.shape)] * 2 + [whole(*w_own.shape)] * 2 + [pl.BlockSpec((1, 256), lambda i: (0, i))],
        out_specs=rows,
        scratch_shapes=[pltpu.VMEM(dk.shape, BF)],
        compiler_params=params(),
        cost_estimate=cost(3 * tokens * width * width, 16 * tokens * width),
        name="input_gradient",
    )(res, got, dq, dk, dv, w_own, w_oth, place)


def after(values, *others):
    return lax.optimization_barrier((values,) + others)[0]


def two_halves(values):
    high = values.astype(BF)
    return jnp.concatenate([high, (values - high.astype(F32)).astype(BF)], axis=0)


def one_value(halves):
    rows = halves.shape[0] // 2
    return halves[:rows].astype(F32) + halves[rows:].astype(F32)


def take(values, which):
    return lax.dynamic_index_in_dim(values, which, 0, False)


def in_order(mine, theirs, which):
    return jnp.concatenate([jnp.where(which == 0, mine, theirs), jnp.where(which == 0, theirs, mine)])


def sum_gradients(sent, kept, mid, input_grad, devices):
    index = lax.axis_index("dp")
    core, near = lax.rem(index, 2), lax.rem(index // 2, 2)
    rows = (sent.shape[0] - 64) // 2

    def across(values, bit):
        return lax.ppermute(values, "dp", [(i, i ^ bit) for i in range(devices)])

    got = across(sent, 1)
    halves = mid.reshape(2, mid.shape[0] // 2, -1)
    mid_got = across(take(halves, 1 - core).astype(BF), 1)
    total = kept[: 2 * rows].astype(F32) + got[: 2 * rows].astype(F32)
    small_own = one_value(kept[2 * rows : 2 * rows + 32]) + one_value(got[2 * rows : 2 * rows + 32])
    small_oth = one_value(kept[2 * rows + 32 :]) + one_value(got[2 * rows + 32 :])
    mid = (take(halves, core) + mid_got.astype(F32)).astype(BF)
    oth_two = two_halves(small_oth)
    mid_got = across(after(mid, oth_two), 4)
    result = input_grad(got)

    own_two = two_halves(small_own)
    got = lax.ppermute(jnp.concatenate([total[rows:].astype(BF), oth_two]), "tensor", [(0, 1), (1, 0)])
    total = total[:rows] + got[:rows].astype(F32)
    small = one_value(own_two) + one_value(got[rows:])

    halves = total.reshape(2, rows // 2, -1)
    two = two_halves(small)
    got = across(jnp.concatenate([take(halves, 1 - near).astype(BF), two]), 2)
    total = take(halves, near) + got[: rows // 2].astype(F32)
    small = one_value(two) + one_value(got[rows // 2 :])

    bit = 4
    while bit < devices:
        sent = jnp.concatenate([total.astype(BF), two_halves(small)])
        mid = (mid.astype(F32) + mid_got.astype(F32)).astype(BF)
        if 2 * bit < devices:
            mid_got = across(mid, 2 * bit)
        got = across(sent, bit)
        total = sent[: rows // 2].astype(F32) + got[: rows // 2].astype(F32)
        small = one_value(sent[rows // 2 :]) + one_value(got[rows // 2 :])
        bit *= 2
    mid = in_order(mid, across(mid, 1), core)
    mid = in_order(after(mid, got), after(across(mid, 2), got), near)

    total = total.astype(BF)
    total = in_order(total, across(total, 2), near)
    total = in_order(total, across(total, 1), core)
    return total.astype(F32), small, mid.astype(F32), result


def mask_parts(known, lengths, halves):
    tokens, slots = known.shape[0] // halves, lengths.shape[0]
    positions = jnp.arange(known.shape[0], dtype=jnp.int32)
    ends = jnp.cumsum(lengths)
    starts = ends - lengths
    inside = (positions[:, None] >= starts[None, :]) & (positions[:, None] < ends[None, :])
    opening = jnp.any((positions[:, None] == starts[None, :]) & (lengths[None, :] > 0), axis=1)
    live = ((known > 0) | opening).astype(jnp.int32).reshape(halves, 1, tokens)
    place = jnp.where(live > 0, jnp.cumsum(live, axis=2) - 1, -1)
    counts = jnp.sum(live, axis=2)
    before = lambda ats: jnp.sum(
        jnp.where(positions.reshape(halves, 1, tokens) < ats[None, :, None], live, 0), axis=2
    )
    past = jnp.full((halves, LANES - HD - slots - 1), tokens, jnp.int32)
    none = jnp.full((halves, HD), tokens, jnp.int32)
    low = jnp.concatenate([none, before(starts), counts, past], axis=1)
    high = jnp.concatenate([none, before(ends), jnp.full((halves, 1), tokens, jnp.int32), past], axis=1)
    queries = jnp.where(jnp.pad(inside, ((0, 0), (0, 1))), 0.0, -MASK_BIG)
    queries = jnp.pad(queries, ((0, 0), (0, HD - slots - 1))).T.astype(BF)
    return place, jnp.stack([low, high], axis=1), queries, jnp.max(counts)


def local(
    devices, layer_input, gene_known, cell_genes, w_qkv, bias_qv, w_out, b_out, ln1_gain, ln1_bias,
    w_up, b_up, w_down, b_down, ln2_gain, ln2_bias, cotangent,
):
    tokens, width = layer_input.shape
    shard = w_qkv.shape[2]
    side, index = lax.axis_index("tensor"), lax.axis_index("dp")
    core, near = lax.rem(index, 2), lax.rem(index // 2, 2)

    def swapped(values):
        return lax.ppermute(values, "tensor", [(0, 1), (1, 0)])

    def across(values, bit):
        return lax.ppermute(values, "dp", [(i, i ^ bit) for i in range(devices)])

    w_own = w_qkv.transpose(1, 0, 2)
    quarter = 3 * width // 4
    mine = lax.dynamic_slice_in_dim(w_own.reshape(3 * width, shard), (2 * core + near) * quarter, quarter, 0)
    got = swapped(jnp.concatenate([mine, jnp.pad(bias_qv, ((0, 14), (0, 0)))]))
    x_oth = swapped(layer_input)
    piece = got[:quarter]
    piece = in_order(piece, across(piece, 2), near)
    w_oth = in_order(piece, across(piece, 1), core).reshape(3, width, shard)
    bias = jnp.concatenate([bias_qv, got[quarter : quarter + 2]], axis=1).astype(F32)

    place, bounds, query_rows, most = mask_parts(gene_known, cell_genes[0], 2)
    query_own = lax.dynamic_slice_in_dim(query_rows, side * tokens, tokens, 1)
    place_own, place_oth, bounds_own, bounds_oth = take(place, side), take(place, 1 - side), take(bounds, side), take(bounds, 1 - side)
    live = jnp.stack([core, most])
    b_up_row = jnp.pad(b_up[None], ((0, 15), (0, shard)))
    mid_w = jnp.concatenate([w_out, w_down, jnp.concatenate([w_up[:shard], w_up[shard:]], axis=1), b_up_row])
    vectors = jnp.stack([b_out, ln1_gain, ln1_bias, b_down, ln2_gain, ln2_bias, b_out, b_out])

    k_own, v_own, x_live, qt, q = project(layer_input, w_own, w_oth, bias, place_own, bounds_own, query_own)
    x_oth, k_own, mid_w = lax.optimization_barrier((x_oth, k_own, mid_w))
    mid_w_oth = swapped(mid_w)
    probs, ot, linv, k_oth, v_oth, x_oth = attend(
        live, qt, k_own, v_own, x_oth, w_own, w_oth, bias, place_oth, bounds_oth
    )
    activations, res, dot_turned, dnat, mid_own, mid_oth, small = middle(
        layer_input, cotangent, ot, linv, mid_w, mid_w_oth, vectors
    )
    mid_got = swapped(mid_oth)
    dq, dx_oth, sums, value_grad = attend_backward(
        1, (live, place_oth), probs, dot_turned, dnat, q, k_oth, v_oth, x_oth, w_own, w_oth
    )
    mid_got, dq = lax.optimization_barrier((mid_got, dq))
    mid = (mid_own + mid_got.astype(F32)).reshape(2, 3 * shard // 2, width)
    mid_got = across(take(mid, 1 - near).astype(BF), 2)
    dx_got = swapped(dx_oth)
    sent, kept, dq, dk, dv = attend_backward(
        0, (live, small, value_grad), probs, dot_turned, dnat, q, k_own, v_own, x_live, dq, sums, layer_input
    )
    mid_got, dx_got, sent = lax.optimization_barrier((mid_got, dx_got, sent))
    mid = take(mid, near) + mid_got.astype(F32)

    def input_grad(token):
        return input_gradient(res, dx_got, after(dq, token), dk, dv, w_own, w_oth, place_own)

    qkv, small, mid, input_grad = sum_gradients(sent, kept, mid, input_grad, devices)
    qkv_g = qkv.reshape(3, width, shard).transpose(1, 0, 2)
    wide = jnp.concatenate([small[:6], small[8:14]], axis=1)
    up_g = jnp.concatenate([mid[width:, :shard], mid[width:, shard:]])
    return (
        activations, input_grad, qkv_g, jnp.stack([small[7], small[15]]), mid[:shard], wide[0], wide[1], wide[2],
        up_g, small[6], mid[shard:width], wide[3], wide[4], wide[5],
    )


def solution(mesh):
    placed = (
        P(("dp", "tensor"), None),
        P("dp"),
        P("dp", None),
        P(None, None, "tensor"),
        P(None, "tensor"),
        P("tensor", None),
        P(),
        P(),
        P(),
        P(None, "tensor"),
        P("tensor"),
        P("tensor", None),
        P(),
        P(),
        P(),
        P(("dp", "tensor"), None),
    )
    return jax.shard_map(
        functools.partial(local, mesh.shape["dp"]),
        mesh=mesh,
        in_specs=placed,
        out_specs=(
            P(("dp", "tensor"), None),
            P(("dp", "tensor"), None),
            P(None, None, "tensor"),
            P(None, "tensor"),
            P("tensor", None),
            P(),
            P(),
            P(),
            P(None, "tensor"),
            P("tensor"),
            P("tensor", None),
            P(),
            P(),
            P(),
        ),
        check_vma=False,
    )
```

profile of v0, /device:TPU:0, one launch (start us, length us, event | category | flops | bytes accessed | tf_op | source)
XLA Modules:
  0.0 178.4 jit_solution(6743295233556028375)
XLA Ops:
  0.7 0.9 constant_dynamic-slice_fusion.4
  1.6 0.7 fusion.6
  2.4 3.0 %collective-permute-start = (bf16[400,256]{1,0:T(8,128)(2,1)S(1)}, bf16[400,256]{1,0:T(8,128)(2,1)S(1)}, u32[]{:S(2)}, u32[]{:S(2)}) collective-permute-start(bf16[400,256]{1,0:T(8,128)(2,1)S(1)} %fusion.6), channel_id=1, source_target_pairs={{0,1},{1,0},{2,3},{3,2},{4,5},{5,4},{6,7},{7,6},{8,9},{9,8},{10,11... | collective-permute-start | bytes 614408 | tf_op jit(solution)/shard_map/ppermute | solution.py:828
  5.5 0.7 compare_bitcast_fusion
  6.2 0.8 reduce-window.10
  7.0 0.7 fusion.28
  7.7 0.7 bitcast_subtract_fusion
  8.5 0.7 broadcast_compare_fusion
  10.9 0.7 fusion.9.extra_q_ref
  11.6 0.6 dynamic-slice_bitcast_fusion
  12.2 1.0 fusion.32
  13.2 2.0 %collective-permute-start.1 = (bf16[384,256]{1,0:T(8,128)(2,1)S(1)}, bf16[384,256]{1,0:T(8,128)(2,1)S(1)}, u32[]{:S(2)}, u32[]{:S(2)}) collective-permute-start(bf16[384,256]{1,0:T(8,128)(2,1)S(1)} %slice.205), channel_id=1, source_target_pairs={{0,4},{2,6},{4,0},{6,2},{8,12},{10,14},{12,8},{14,10},{16,20},{18,... | collective-permute-start | bytes 589832 | tf_op jit(solution)/shard_map/ppermute | solution.py:831
  15.3 4.4 %collective-permute-done.1 = bf16[384,256]{1,0:T(8,128)(2,1)S(1)} collective-permute-done((bf16[384,256]{1,0:T(8,128)(2,1)S(1)}, bf16[384,256]{1,0:T(8,128)(2,1)S(1)}, u32[]{:S(2)}, u32[]{:S(2)}) %collective-permute-start.1) | collective-permute-done | bytes 196640 | tf_op jit(solution)/shard_map/ppermute | solution.py:831
  20.4 0.6 reduce_max.9
  21.0 1.2 pad_add_fusion.live_ref.refs_0_
  22.3 0.6 stack.56.vec_ref
  23.0 0.7 maximum_convert_fusion.4.bias_ref
  23.9 1.0 pad_maximum_fusion
  24.9 8.4 %project.1 = (bf16[8,1024,128]{2,1,0:T(8,128)(2,1)}, bf16[8,1024,128]{2,1,0:T(8,128)(2,1)}, bf16[1024,512]{1,0:T(8,128)(2,1)}, bf16[8,128,1024]{2,1,0:T(8,128)(2,1)}, bf16[1024,512]{1,0:T(8,128)(2,1)}) custom-call(bf16[1024,512]{1,0:T(8,128)(2,1)} %refs_12_.1, bf16[3,512,256]{2,1,0:T(8,128)(2,1)} %bitcast.89, bf16[3,512,256]{2,1,0:T(8,128)(2,1)} %bitcast.79, ...), custom_call_target="tpu_custom_call" | custom-call | flops 2684354560 | bytes 6291456 | tf_op jit(solution)/shard_map/project/pallas_call | solution.py:96
  33.3 1.7 collective-permute-start.4
  35.0 23.0 %attend.1 = (bf16[8,2048,1024]{2,1,0:T(8,128)(2,1)}, f32[8,64,1024]{2,1,0:T(8,128)}, f32[8,1,1024]{2,1,0:T(1,128)}, bf16[8,1024,128]{2,1,0:T(8,128)(2,1)}, bf16[...) custom-call(s32[2]{0:T(128)} %pad_add_fusion.live_ref.refs_0_, bf16[8,128,1024]{2,1,0:T(8,128)(2,1)} %get-tuple-element.52.qt_hbm, ...), custom_call_target="tpu_custom_call" | custom-call | flops 17179869184 | bytes 33554432 | tf_op jit(solution)/shard_map/attend/pallas_call | solution.py:282
  58.1 0.9 copy-done.14
  59.0 13.6 %middle.1 = (bf16[1024,512]{1,0:T(8,128)(2,1)}, f32[1024,512]{1,0:T(8,128)}, bf16[8,128,1024]{2,1,0:T(8,128)(2,1)}, bf16[1024,512]{1,0:T(8,128)(2,1)}, f32[768,5...) custom-call(bf16[1024,512]{1,0:T(8,128)(2,1)} %refs_12_.1, bf16[1024,512]{1,0:T(8,128)(2,1)} %cot_ref.1, ...), custom_call_target="tpu_custom_call" | custom-call | flops 4831838208 | bytes 10485760 | tf_op jit(solution)/shard_map/middle/pallas_call | solution.py:433
  72.6 1.0 collective-permute-start.5
  73.6 23.5 %attend_back_other.1 = (f32[512,1024]{1,0:T(8,128)}, bf16[1024,512]{1,0:T(8,128)(2,1)}, f32[2,512,512]{2,1,0:T(8,128)}, f32[2,512]{1,0:T(2,128)}) custom-call(s32[2]{0:T(128)} %pad_add_fusion.live_ref.refs_0_, s32[1,1024]{1,0:T(1,128)} %get-tuple-element.129.place_ref.refs_1_, bf16[8,2048,1024]{2,1,0:T(8,128)(2,1)} %get-tuple-element.64.refs_2_.refs_3_, ...), custom_call_target="tpu_custom_call" | custom-call | flops 17179869184 | bytes 16777216 | tf_op jit(solution)/shard_map/attend_back_other/pallas_call | solution.py:674
  97.1 1.2 collective-permute-start.7
  98.6 1.6 collective-permute-start.6
  100.2 23.4 %attend_back_own.1 = (bf16[1600,256]{1,0:T(8,128)(2,1)}, bf16[1600,256]{1,0:T(8,128)(2,1)}, bf16[1024,512]{1,0:T(8,128)(2,1)}, bf16[1024,512]{1,0:T(8,128)(2,1)}, bf16[1024,512]{1,0:T(8,128)(2,1)}) custom-call(s32[2]{0:T(128)} %pad_add_fusion.live_ref.refs_0_, f32[8,512]{1,0:T(8,128)} %get-tuple-element.74.refs_1_, f32[2,512]{1,0:T(2,128)} %get-tuple-element.75.refs_2_, ...), custom_call_target="tpu_custom_call" | custom-call | flops 17179869184 | bytes 16777216 | tf_op jit(solution)/shard_map/attend_back_own/pallas_call | solution.py:674
  123.7 1.4 bitcast_add_fusion
  125.4 1.2 collective-permute-done.15
  126.7 1.6 collective-permute-start.16
  128.4 1.3 convert_add_fusion
  129.7 0.7 subtract_convert_fusion
  130.5 1.0 collective-permute-start.9
  131.5 2.3 %collective-permute-done.16 = bf16[192,512]{1,0:T(8,128)(2,1)S(1)} collective-permute-done((bf16[192,512]{1,0:T(8,128)(2,1)S(1)}, bf16[192,512]{1,0:T(8,128)(2,1)S(1)}, u32[]{:S(2)}, u32[]{:S(2)}) %collective-permute-start.16) | collective-permute-done | bytes 196640 | tf_op jit(solution)/shard_map/ppermute | solution.py:753
  133.9 2.7 %collective-permute-start.17 = (bf16[192,512]{1,0:T(8,128)(2,1)S(1)}, bf16[192,512]{1,0:T(8,128)(2,1)S(1)}, u32[]{:S(2)}, u32[]{:S(2)}) collective-permute-start(bf16[192,512]{1,0:T(8,128)(2,1)S(1)} %add_convert_fusion.1), channel_id=1, source_target_pairs={{0,16},{2,18},{4,20},{6,22},{8,24},{10,26},{12,28},{14,30},{16,0},... | collective-permute-start | bytes 589832 | tf_op jit(solution)/shard_map/ppermute | solution.py:753
  136.5 5.3 %collective-permute-done.9 = bf16[800,256]{1,0:T(8,128)(2,1)S(1)} collective-permute-done((bf16[800,256]{1,0:T(8,128)(2,1)S(1)}, bf16[800,256]{1,0:T(8,128)(2,1)S(1)}, u32[]{:S(2)}, u32[]{:S(2)}) %collective-permute-start.9) | collective-permute-done | bytes 409632 | tf_op jit(solution)/shard_map/ppermute | solution.py:767
  141.9 0.7 fusion.15
  143.3 1.9 %collective-permute-done.17 = bf16[192,512]{1,0:T(8,128)(2,1)S(1)} collective-permute-done((bf16[192,512]{1,0:T(8,128)(2,1)S(1)}, bf16[192,512]{1,0:T(8,128)(2,1)S(1)}, u32[]{:S(2)}, u32[]{:S(2)}) %collective-permute-start.17) | collective-permute-done | bytes 196640 | tf_op jit(solution)/shard_map/ppermute | solution.py:753
  145.4 3.6 %collective-permute-done.10 = bf16[416,256]{1,0:T(8,128)(2,1)S(1)} collective-permute-done((bf16[416,256]{1,0:T(8,128)(2,1)S(1)}, bf16[416,256]{1,0:T(8,128)(2,1)S(1)}, u32[]{:S(2)}, u32[]{:S(2)}) %collective-permute-start.10) | collective-permute-done | bytes 213024 | tf_op jit(solution)/shard_map/ppermute | solution.py:753
  150.3 4.7 %collective-permute-done.11 = bf16[416,256]{1,0:T(8,128)(2,1)S(1)} collective-permute-done((bf16[416,256]{1,0:T(8,128)(2,1)S(1)}, bf16[416,256]{1,0:T(8,128)(2,1)S(1)}, u32[]{:S(2)}, u32[]{:S(2)}) %collective-permute-start.11) | collective-permute-done | bytes 213024 | tf_op jit(solution)/shard_map/ppermute | solution.py:753
  155.1 4.2 %collective-permute-start.12 = (bf16[416,256]{1,0:T(8,128)(2,1)S(1)}, bf16[416,256]{1,0:T(8,128)(2,1)S(1)}, u32[]{:S(2)}, u32[]{:S(2)}) collective-permute-start(bf16[416,256]{1,0:T(8,128)(2,1)S(1)} %pad_maximum_fusion.9), channel_id=1, source_target_pairs={{0,16},{2,18},{4,20},{6,22},{8,24},{10,26},{12,28},{14,30},{16,0},... | collective-permute-start | bytes 638984 | tf_op jit(solution)/shard_map/ppermute | solution.py:753
  159.3 8.4 %input_gradient.1 = f32[1024,512]{1,0:T(8,128)} custom-call(f32[1024,512]{1,0:T(8,128)} %get-tuple-element.61.res_ref, bf16[1024,512]{1,0:T(8,128)(2,1)} %copy-done.1, bf16[1024,512]{1,0:T(8,128)(2,1)} %get-tuple-element.83.dq_ref, bf16[1024,512]{1,0:T(8,128)(2,1)} %get-tuple-element.84.dk_ref, bf16[1024,512]{1,0:T(8,128)(2,1)} %get-tuple-element.85.dv_ref, ...), custom_call_target="tpu_custom_call" | custom-call | flops 1610612736 | bytes 8388608 | tf_op jit(solution)/shard_map/input_gradient/pallas_call | solution.py:712
  169.9 3.7 %collective-permute-done.13 = bf16[384,256]{1,0:T(8,128)(2,1)S(1)} collective-permute-done((bf16[384,256]{1,0:T(8,128)(2,1)S(1)}, bf16[384,256]{1,0:T(8,128)(2,1)S(1)}, u32[]{:S(2)}, u32[]{:S(2)}) %collective-permute-start.13) | collective-permute-done | bytes 196640 | tf_op jit(solution)/shard_map/ppermute | solution.py:753
  174.3 0.8 slice.229
  175.2 0.9 maximum_convert_fusion.1
  176.1 0.8 pad_maximum_fusion.2
  177.1 1.3 convert_bitcast_fusion
  (115 shorter events, 9.1 us)
Async XLA Ops:
  2.3 19.9 %copy-start.15 = (bf16[256]{0:T(256)(128)(2,1)S(1)}, bf16[256]{0:T(256)(128)(2,1)}, u32[]{:S(2)}) copy-start(bf16[256]{0:T(256)(128)(2,1)} %param.26) | copy-start | bytes 1540
  2.3 19.9 %copy-start.6 = (f32[512]{0:T(512)S(1)}, f32[512]{0:T(512)}, u32[]{:S(2)}) copy-start(f32[512]{0:T(512)} %param.22) | copy-start | bytes 6148
  2.3 19.9 %copy-start.8 = (f32[512]{0:T(512)S(1)}, f32[512]{0:T(512)}, u32[]{:S(2)}) copy-start(f32[512]{0:T(512)} %param.23) | copy-start | bytes 6148
  2.4 19.9 %copy-start.9 = (f32[512]{0:T(512)S(1)}, f32[512]{0:T(512)}, u32[]{:S(2)}) copy-start(f32[512]{0:T(512)} %param.24) | copy-start | bytes 6148
  2.4 19.9 %copy-start.10 = (f32[512]{0:T(512)S(1)}, f32[512]{0:T(512)}, u32[]{:S(2)}) copy-start(f32[512]{0:T(512)} %param.28) | copy-start | bytes 6148
  2.4 19.9 %copy-start.11 = (f32[512]{0:T(512)S(1)}, f32[512]{0:T(512)}, u32[]{:S(2)}) copy-start(f32[512]{0:T(512)} %param.29) | copy-start | bytes 6148
  2.4 19.9 %copy-start.12 = (f32[512]{0:T(512)S(1)}, f32[512]{0:T(512)}, u32[]{:S(2)}) copy-start(f32[512]{0:T(512)} %param.30) | copy-start | bytes 6148
  2.4 20.5 %copy-start.4 = (bf16[256,512]{1,0:T(8,128)(2,1)S(1)}, bf16[256,512]{1,0:T(8,128)(2,1)}, u32[]{:S(2)}) copy-start(bf16[256,512]{1,0:T(8,128)(2,1)} %param.27) | copy-start | bytes 786436
  2.4 20.5 %copy-start.5 = (bf16[256,512]{1,0:T(8,128)(2,1)S(1)}, bf16[256,512]{1,0:T(8,128)(2,1)}, u32[]{:S(2)}) copy-start(bf16[256,512]{1,0:T(8,128)(2,1)} %param.21) | copy-start | bytes 786436
  2.4 10.8 %collective-permute-start = (bf16[400,256]{1,0:T(8,128)(2,1)S(1)}, bf16[400,256]{1,0:T(8,128)(2,1)S(1)}, u32[]{:S(2)}, u32[]{:S(2)}) collective-permute-start(bf16[400,256]{1,0:T(8,128)(2,1)S(1)} %fusion.6), channel_id=1, source_target_pairs={{0,1},{1,0},{2,3},{3,2},{4,5},{5,4},{6,7},{7,6},{8,9},{9,8},{10,11... | collective-permute-start | bytes 614408 | tf_op jit(solution)/shard_map/ppermute | solution.py:828
  5.5 27.8 %collective-permute-start.3 = (bf16[1024,512]{1,0:T(8,128)(2,1)}, bf16[1024,512]{1,0:T(8,128)(2,1)S(1)}, u32[]{:S(2)}, u32[]{:S(2)}) collective-permute-start(bf16[1024,512]{1,0:T(8,128)(2,1)} %refs_12_.1), channel_id=1, source_target_pairs={{0,1},{1,0},{2,3},{3,2},{4,5},{5,4},{6,7},{7,6},{8,9},{9,8},{10,11... | collective-permute-start | bytes 3145736 | tf_op jit(solution)/shard_map/ppermute | solution.py:828
  13.2 6.4 %collective-permute-start.1 = (bf16[384,256]{1,0:T(8,128)(2,1)S(1)}, bf16[384,256]{1,0:T(8,128)(2,1)S(1)}, u32[]{:S(2)}, u32[]{:S(2)}) collective-permute-start(bf16[384,256]{1,0:T(8,128)(2,1)S(1)} %slice.205), channel_id=1, source_target_pairs={{0,4},{2,6},{4,0},{6,2},{8,12},{10,14},{12,8},{14,10},{16,20},{18,... | collective-permute-start | bytes 589832 | tf_op jit(solution)/shard_map/ppermute | solution.py:831
  15.3 7.7 %copy-start.7 = (bf16[2,256]{1,0:T(2,128)(2,1)S(1)}, bf16[2,256]{1,0:T(2,128)(2,1)}, u32[]{:S(2)}) copy-start(bf16[2,256]{1,0:T(2,128)(2,1)} %param.20) | copy-start | bytes 3076
  19.7 4.0 %collective-permute-start.2 = (bf16[768,256]{1,0:T(8,128)(2,1)S(1)}, bf16[768,256]{1,0:T(8,128)(2,1)S(1)}, u32[]{:S(2)}, u32[]{:S(2)}) collective-permute-start(bf16[768,256]{1,0:T(8,128)(2,1)S(1)} %pad_maximum_fusion.4), channel_id=1, source_target_pairs={{0,2},{2,0},{4,6},{6,4},{8,10},{10,8},{12,14},{14,12},{16,18},{18,... | collective-permute-start | bytes 1179656 | tf_op jit(solution)/shard_map/ppermute | solution.py:831
  23.0 10.3 %copy-start.3 = (bf16[784,512]{1,0:T(8,128)(2,1)}, bf16[784,512]{1,0:T(8,128)(2,1)S(1)}, u32[]{:S(2)}) copy-start(bf16[784,512]{1,0:T(8,128)(2,1)S(1)} %fusion.1.w_own_ref) | copy-start | bytes 2408452
  33.3 1.8 copy-start.13
  33.3 24.8 %collective-permute-start.4 = (bf16[784,512]{1,0:T(8,128)(2,1)S(1)}, bf16[784,512]{1,0:T(8,128)(2,1)S(1)}, u32[]{:S(2)}, u32[]{:S(2)}) collective-permute-start(bf16[784,512]{1,0:T(8,128)(2,1)S(1)} %fusion.1.w_own_ref), channel_id=1, source_target_pairs={{0,1},{1,0},{2,3},{3,2},{4,5},{5,4},{6,7},{7,6},{8,9},{9,8},{10,11... | collective-permute-start | bytes 2408456 | tf_op jit(solution)/shard_map/ppermute | solution.py:828
  58.1 0.9 copy-start.14
  72.6 25.7 %collective-permute-start.5 = (bf16[768,512]{1,0:T(8,128)(2,1)}, bf16[768,512]{1,0:T(8,128)(2,1)S(1)}, u32[]{:S(2)}, u32[]{:S(2)}) collective-permute-start(bf16[768,512]{1,0:T(8,128)(2,1)} %get-tuple-element.63), channel_id=1, source_target_pairs={{0,1},{1,0},{2,3},{3,2},{4,5},{5,4},{6,7},{7,6},{8,9},{9,8},{10,11... | collective-permute-start | bytes 2359304 | tf_op jit(solution)/shard_map/ppermute | solution.py:828
  73.6 24.7 %copy-start = (f32[768,512]{1,0:T(8,128)S(1)}, f32[768,512]{1,0:T(8,128)}, u32[]{:S(2)}) copy-start(f32[768,512]{1,0:T(8,128)} %get-tuple-element.62) | copy-start | bytes 4718596
  97.1 26.5 %collective-permute-start.7 = (bf16[1024,512]{1,0:T(8,128)(2,1)}, bf16[1024,512]{1,0:T(8,128)(2,1)S(1)}, u32[]{:S(2)}, u32[]{:S(2)}) collective-permute-start(bf16[1024,512]{1,0:T(8,128)(2,1)} %get-tuple-element.73), channel_id=1, source_target_pairs={{0,1},{1,0},{2,3},{3,2},{4,5},{5,4},{6,7},{7,6},{8,9},{9,8},{10,11... | collective-permute-start | bytes 3145736 | tf_op jit(solution)/shard_map/ppermute | solution.py:828
  98.6 25.0 %collective-permute-start.6 = (bf16[384,512]{1,0:T(8,128)(2,1)S(1)}, bf16[384,512]{1,0:T(8,128)(2,1)}, u32[]{:S(2)}, u32[]{:S(2)}) collective-permute-start(bf16[384,512]{1,0:T(8,128)(2,1)S(1)} %fusion.3), channel_id=1, source_target_pairs={{0,4},{2,6},{4,0},{6,2},{8,12},{10,14},{12,8},{14,10},{16,20},{18,... | collective-permute-start | bytes 1179656 | tf_op jit(solution)/shard_map/ppermute | solution.py:831
  123.6 3.1 %copy-start.1 = (bf16[1024,512]{1,0:T(8,128)(2,1)}, bf16[1024,512]{1,0:T(8,128)(2,1)S(1)}, u32[]{:S(2)}) copy-start(bf16[1024,512]{1,0:T(8,128)(2,1)S(1)} %collective-permute-done.7.got_ref) | copy-start | bytes 3145732
  123.6 4.7 %collective-permute-start.8 = (bf16[1600,256]{1,0:T(8,128)(2,1)}, bf16[1600,256]{1,0:T(8,128)(2,1)}, u32[]{:S(2)}, u32[]{:S(2)}) collective-permute-start(bf16[1600,256]{1,0:T(8,128)(2,1)} %get-tuple-element.82), channel_id=1, source_target_pairs={{0,2},{2,0},{4,6},{6,4},{8,10},{10,8},{12,14},{14,12},{16,18},{18,... | collective-permute-start | bytes 2457608 | tf_op jit(solution)/shard_map/ppermute | solution.py:753
  125.1 3.3 %copy-start.2 = (bf16[1600,256]{1,0:T(8,128)(2,1)S(1)}, bf16[1600,256]{1,0:T(8,128)(2,1)}, u32[]{:S(2)}) copy-start(bf16[1600,256]{1,0:T(8,128)(2,1)} %get-tuple-element.86) | copy-start | bytes 2457604
  125.2 1.5 collective-permute-start.15
  126.7 7.1 %collective-permute-start.16 = (bf16[192,512]{1,0:T(8,128)(2,1)S(1)}, bf16[192,512]{1,0:T(8,128)(2,1)S(1)}, u32[]{:S(2)}, u32[]{:S(2)}) collective-permute-start(bf16[192,512]{1,0:T(8,128)(2,1)S(1)} %fusion.4), channel_id=1, source_target_pairs={{0,8},{2,10},{4,12},{6,14},{8,0},{10,2},{12,4},{14,6},{16,24},{18,... | collective-permute-start | bytes 589832 | tf_op jit(solution)/shard_map/ppermute | solution.py:753
  130.5 11.4 %collective-permute-start.9 = (bf16[800,256]{1,0:T(8,128)(2,1)S(1)}, bf16[800,256]{1,0:T(8,128)(2,1)S(1)}, u32[]{:S(2)}, u32[]{:S(2)}) collective-permute-start(bf16[800,256]{1,0:T(8,128)(2,1)S(1)} %pad_maximum_fusion.3), channel_id=1, source_target_pairs={{0,1},{1,0},{2,3},{3,2},{4,5},{5,4},{6,7},{7,6},{8,9},{9,8},{10,11... | collective-permute-start | bytes 1228808 | tf_op jit(solution)/shard_map/ppermute | solution.py:767
  133.9 11.4 %collective-permute-start.17 = (bf16[192,512]{1,0:T(8,128)(2,1)S(1)}, bf16[192,512]{1,0:T(8,128)(2,1)S(1)}, u32[]{:S(2)}, u32[]{:S(2)}) collective-permute-start(bf16[192,512]{1,0:T(8,128)(2,1)S(1)} %add_convert_fusion.1), channel_id=1, source_target_pairs={{0,16},{2,18},{4,20},{6,22},{8,24},{10,26},{12,28},{14,30},{16,0},... | collective-permute-start | bytes 589832 | tf_op jit(solution)/shard_map/ppermute | solution.py:753
  142.7 6.3 %collective-permute-start.10 = (bf16[416,256]{1,0:T(8,128)(2,1)S(1)}, bf16[416,256]{1,0:T(8,128)(2,1)S(1)}, u32[]{:S(2)}, u32[]{:S(2)}) collective-permute-start(bf16[416,256]{1,0:T(8,128)(2,1)S(1)} %pad_maximum_fusion.7), channel_id=1, source_target_pairs={{0,4},{2,6},{4,0},{6,2},{8,12},{10,14},{12,8},{14,10},{16,20},{18,... | collective-permute-start | bytes 638984 | tf_op jit(solution)/shard_map/ppermute | solution.py:753
  145.3 4.3 %collective-permute-start.18 = (bf16[192,512]{1,0:T(8,128)(2,1)S(1)}, bf16[192,512]{1,0:T(8,128)(2,1)S(1)}, u32[]{:S(2)}, u32[]{:S(2)}) collective-permute-start(bf16[192,512]{1,0:T(8,128)(2,1)S(1)} %add_convert_fusion), channel_id=1, source_target_pairs={{0,2},{2,0},{4,6},{6,4},{8,10},{10,8},{12,14},{14,12},{16,18},{18,... | collective-permute-start | bytes 589832 | tf_op jit(solution)/shard_map/ppermute | solution.py:753
  149.1 5.9 %collective-permute-start.11 = (bf16[416,256]{1,0:T(8,128)(2,1)S(1)}, bf16[416,256]{1,0:T(8,128)(2,1)S(1)}, u32[]{:S(2)}, u32[]{:S(2)}) collective-permute-start(bf16[416,256]{1,0:T(8,128)(2,1)S(1)} %pad_maximum_fusion.8), channel_id=1, source_target_pairs={{0,8},{2,10},{4,12},{6,14},{8,0},{10,2},{12,4},{14,6},{16,24},{18,... | collective-permute-start | bytes 638984 | tf_op jit(solution)/shard_map/ppermute | solution.py:753
  149.7 18.1 %collective-permute-start.19 = (bf16[384,512]{1,0:T(8,128)(2,1)S(1)}, bf16[384,512]{1,0:T(8,128)(2,1)S(1)}, u32[]{:S(2)}, u32[]{:S(2)}) collective-permute-start(bf16[384,512]{1,0:T(8,128)(2,1)S(1)} %pad_maximum_fusion.6), channel_id=1, source_target_pairs={{0,4},{2,6},{4,0},{6,2},{8,12},{10,14},{12,8},{14,10},{16,20},{18,... | collective-permute-start | bytes 1179656 | tf_op jit(solution)/shard_map/ppermute | solution.py:753
  155.1 12.6 %collective-permute-start.12 = (bf16[416,256]{1,0:T(8,128)(2,1)S(1)}, bf16[416,256]{1,0:T(8,128)(2,1)S(1)}, u32[]{:S(2)}, u32[]{:S(2)}) collective-permute-start(bf16[416,256]{1,0:T(8,128)(2,1)S(1)} %pad_maximum_fusion.9), channel_id=1, source_target_pairs={{0,16},{2,18},{4,20},{6,22},{8,24},{10,26},{12,28},{14,30},{16,0},... | collective-permute-start | bytes 638984 | tf_op jit(solution)/shard_map/ppermute | solution.py:753
  167.9 5.7 %collective-permute-start.13 = (bf16[384,256]{1,0:T(8,128)(2,1)S(1)}, bf16[384,256]{1,0:T(8,128)(2,1)S(1)}, u32[]{:S(2)}, u32[]{:S(2)}) collective-permute-start(bf16[384,256]{1,0:T(8,128)(2,1)S(1)} %add_convert_fusion.2), channel_id=1, source_target_pairs={{0,4},{2,6},{4,0},{6,2},{8,12},{10,14},{12,8},{14,10},{16,20},{18,... | collective-permute-start | bytes 589832 | tf_op jit(solution)/shard_map/ppermute | solution.py:753
  173.7 3.2 %collective-permute-start.14 = (bf16[768,256]{1,0:T(8,128)(2,1)S(1)}, bf16[768,256]{1,0:T(8,128)(2,1)S(1)}, u32[]{:S(2)}, u32[]{:S(2)}) collective-permute-start(bf16[768,256]{1,0:T(8,128)(2,1)S(1)} %pad_maximum_fusion.5), channel_id=1, source_target_pairs={{0,2},{2,0},{4,6},{6,4},{8,10},{10,8},{12,14},{14,12},{16,18},{18,... | collective-permute-start | bytes 1179656 | tf_op jit(solution)/shard_map/ppermute | solution.py:753
where the time goes:
time: 179 us; the launch traced here: 178 us
  Pallas kernels  100 us (56%)
  waiting for transfers between devices  27.3 us (15%)
  starting transfers between devices  22.9 us (13%)
  other arithmetic  19.5 us (11%)
  local copies, waits for them, and re-layouts  7.01 us (4%)
    pallas_call x2, Pallas kernels, attend_backward(): pl.pallas_call(functools.partial(backward_kernel, sub, part), out_shape=o...  46.9 us
    pallas_call x1, Pallas kernels, attend(): pl.pallas_call(functools.partial(attend_kernel, count, chunk), out_shape=...  23 us
    ppermute x14, waiting for transfers between devices, across(): return lax.ppermute(values, 'dp', [(i, i ^ bit) for i in range(devices)])  21.9 us
    ppermute x14, starting transfers between devices, across(): return lax.ppermute(values, 'dp', [(i, i ^ bit) for i in range(devices)])  14.9 us
    pallas_call x1, Pallas kernels, middle(): pl.pallas_call(functools.partial(middle_kernel, sub), grid=(tokens // blo...  13.6 us
    pallas_call x1, Pallas kernels, input_gradient(): pl.pallas_call(input_kernel, grid=(tokens // 256,), out_shape=jax.ShapeDt...  8.44 us
    pallas_call x1, Pallas kernels, project(): pl.pallas_call(project_kernel, grid=(tokens // block,), out_shape=(jax.Sh...  8.41 us
    ppermute x5, starting transfers between devices, swapped(): return lax.ppermute(values, 'tensor', [(0, 1), (1, 0)])  6.98 us
  transfers between devices with their start and end apart: 20, of which 8 were waited for; matrix products, arithmetic and copies ran while one was open for 13% of the time, Pallas kernels for 49%

commit v1 on v0

--- a/solution.py
+++ b/solution.py
@@ -580,12 +580,9 @@
     for_size(live_ref[1], keys, work)
     for copy in last_copies:
         copy.wait()
-    bias_ref[...] = jnp.zeros_like(bias_ref)
     if part:
-        gw_ref[...] = jnp.zeros_like(gw_ref)
         copies_out = [rows_out(p) for p in range(heads // 2)]
     else:
-        gq_ref[...] = jnp.zeros_like(gq_ref)
         copies_out = [
             pltpu.make_async_copy(dk_ref, dk_hbm, out_sem.at[0]),
             pltpu.make_async_copy(dv_ref, dv_hbm, out_sem.at[1]),
@@ -593,38 +590,27 @@
         for copy in copies_out:
             copy.start()
 
-    def weight_sums(size, rolled):
-        def at_rows(at, carry):
-            rows = pl.ds(at, size // 4)
-            x, dk, dv = x_ref[rows, :], dk_ref[rows, :], dv_ref[rows, :]
-            gw_ref[0] += dot(x, dk, 0, 0)
-            gw_ref[1] += dot(x, dv, 0, 0)
-            bias_ref[1:2, :] += jnp.sum(dv.astype(F32), axis=0, keepdims=True)
-            if part:
-                dx = times_weights(dk, own_ref, oth_ref, 1) + times_weights(dv, own_ref, oth_ref, 2)
-                dx_scr[rows, :] = dx.astype(BF)
-            return carry
-
-        def back_in_place(at, carry):
-            rows = pl.ds(at, sub)
-            earlier = size if rolled else min(at + sub, size)
-            dx_ref[rows, :] = dot(live_rows(place_ref, 0, earlier, rows), dx_scr[:earlier, :], 0, 0).astype(BF)
-            return carry
-
-        sweep(True, size, 4, at_rows)
-        if part:
-            sweep(rolled, keys, keys // sub, back_in_place)
-
-    for_size(live_ref[1], keys, weight_sums)
-    if not part:
-
-        @pl.loop(0, queries // sub)
+    for n, grad_ref in enumerate((dk_ref, dv_ref)):
+        grad = dot(x_ref[...], grad_ref[...], 0, 0)
+        gw_ref[n] = grad if part else gw_ref[n] + grad
+    bias_ref[1:2, :] = jnp.sum(dv_ref[...].astype(F32), axis=0, keepdims=True)
+    if part:
+        bias_ref[0:1, :] = jnp.zeros((1, width), F32)
+
+        @pl.loop(0, keys // sub)
         def _(i):
             rows = pl.ds(pl.multiple_of(i * sub, sub), sub)
-            dq = ((before_ref[:, rows] + dq_ref[:, rows]) * HD**-0.5).astype(BF).T
-            dq_out[rows, :] = dq
-            gq_ref[...] += dot(whole_ref[rows, :], dq, 0, 0)
-            bias_ref[0:1, :] += jnp.sum(dq.astype(F32), axis=0, keepdims=True)
+            dk, dv = dk_ref[rows, :], dv_ref[rows, :]
+            dx = times_weights(dk, own_ref, oth_ref, 1) + times_weights(dv, own_ref, oth_ref, 2)
+            dx_scr[rows, :] = dx.astype(BF)
+
+        for at in range(0, keys, sub):
+            rows, earlier = slice(at, at + sub), at + sub
+            dx_ref[rows, :] = dot(live_rows(place_ref, 0, earlier, rows), dx_scr[:earlier, :], 0, 0).astype(BF)
+    else:
+        dq_out[...] = ((before_ref[...] + dq_ref[...]) * HD**-0.5).astype(BF).T
+        gq_ref[...] = dot(whole_ref[...], dq_out[...], 0, 0)
+        bias_ref[0:1, :] = jnp.sum(dq_out[...].astype(F32), axis=0, keepdims=True)
 
     if not part:
         first = live_ref[0] == 0
@@ -692,15 +678,16 @@
 
 
 def input_kernel(res_ref, got_ref, dq_ref, dk_ref, dv_ref, own_ref, oth_ref, place_ref, dx_ref, live_scr):
-    @pl.when(pl.program_id(0) == 0)
+    block = res_ref.shape[0]
+    step = pl.program_id(0)
+
+    @pl.when(step == 0)
     def _():
-        @pl.loop(0, live_scr.shape[0] // 256)
-        def _(i):
-            rows = pl.ds(pl.multiple_of(i * 256, 256), 256)
-            live_scr[rows, :] = (
-                times_weights(dk_ref[rows, :], own_ref, oth_ref, 1) + times_weights(dv_ref[rows, :], own_ref, oth_ref, 2)
-            ).astype(BF)
-
+        live_scr[...] = jnp.zeros_like(live_scr)
+
+    live_scr[pl.ds(pl.multiple_of(step * block, block), block), :] = (
+        times_weights(dk_ref[...], own_ref, oth_ref, 1) + times_weights(dv_ref[...], own_ref, oth_ref, 2)
+    ).astype(BF)
     dx = res_ref[...] + got_ref[...].astype(F32) + times_weights(dq_ref[...], own_ref, oth_ref, 0)
     dx_ref[...] = dx + dot(live_rows(place_ref, 0, live_scr.shape[0]), live_scr[...], 0, 0)
 
@@ -713,7 +700,7 @@
         input_kernel,
         grid=(tokens // 256,),
         out_shape=jax.ShapeDtypeStruct((tokens, width), F32),
-        in_specs=[rows] * 3 + [whole(*dk.shape)] * 2 + [whole(*w_own.shape)] * 2 + [pl.BlockSpec((1, 256), lambda i: (0, i))],
+        in_specs=[rows] * 5 + [whole(*w_own.shape)] * 2 + [pl.BlockSpec((1, 256), lambda i: (0, i))],
         out_specs=rows,
         scratch_shapes=[pltpu.VMEM(dk.shape, BF)],
         compiler_params=params(),
@@ -787,10 +774,14 @@
     mid = in_order(mid, across(mid, 1), core)
     mid = in_order(after(mid, got), after(across(mid, 2), got), near)
 
+    up = mid.shape[0] * 2 // 3
+    mid = mid[:up // 2].astype(F32), mid[up // 2 : up].astype(F32), mid[up:].astype(F32)
+    mid = mid[0], mid[1], jnp.concatenate([mid[2][:, : sent.shape[1]], mid[2][:, sent.shape[1] :]])
+
     total = total.astype(BF)
     total = in_order(total, across(total, 2), near)
     total = in_order(total, across(total, 1), core)
-    return total.astype(F32), small, mid.astype(F32), result
+    return total.astype(F32), small, mid, result
 
 
 def mask_parts(known, lengths, halves):
@@ -877,10 +868,10 @@
     qkv, small, mid, input_grad = sum_gradients(sent, kept, mid, input_grad, devices)
     qkv_g = qkv.reshape(3, width, shard).transpose(1, 0, 2)
     wide = jnp.concatenate([small[:6], small[8:14]], axis=1)
-    up_g = jnp.concatenate([mid[width:, :shard], mid[width:, shard:]])
+    out_g, down_g, up_g = mid
     return (
-        activations, input_grad, qkv_g, jnp.stack([small[7], small[15]]), mid[:shard], wide[0], wide[1], wide[2],
-        up_g, small[6], mid[shard:width], wide[3], wide[4], wide[5],
+        activations, input_grad, qkv_g, jnp.stack([small[7], small[15]]), out_g, wide[0], wide[1], wide[2],
+        up_g, small[6], down_g, wide[3], wide[4], wide[5],
     )
 
 

time: 179 us -> 175 us (0.978)
  starting transfers between devices: 22.9 us -> 25.7 us
  waiting for transfers between devices: 27.3 us -> 24.5 us
  Pallas kernels: 100 us -> 97.6 us
    ppermute x14, waiting for transfers between devices: 21.9 us -> 18.4 us  [across(): return lax.ppermute(values, 'dp', [(i, i ^ bit) for i in range(devices)])]
    ppermute x14, starting transfers between devices: 14.9 us -> 17.7 us  [across(): return lax.ppermute(values, 'dp', [(i, i ^ bit) for i in range(devices)])]
  transfers between devices with their start and end apart: 20 -> 20, of which waited for: 8 -> 10; matrix products, arithmetic and copies ran while one was open for 13% -> 12% of each run, Pallas kernels for 49% -> 48%
where the time goes in v1:
time: 175 us
  Pallas kernels  97.6 us (56%)
  starting transfers between devices  25.7 us (15%)
  waiting for transfers between devices  24.5 us (14%)
  other arithmetic  19.6 us (11%)
  local copies, waits for them, and re-layouts  6.21 us (4%)
    pallas_call x2, Pallas kernels, attend_backward(): pl.pallas_call(functools.partial(backward_kernel, sub, part), out_shape=o...  45.2 us
    pallas_call x1, Pallas kernels, attend(): pl.pallas_call(functools.partial(attend_kernel, count, chunk), out_shape=...  23.1 us
    ppermute x14, waiting for transfers between devices, across(): return lax.ppermute(values, 'dp', [(i, i ^ bit) for i in range(devices)])  18.4 us
    ppermute x14, starting transfers between devices, across(): return lax.ppermute(values, 'dp', [(i, i ^ bit) for i in range(devices)])  17.7 us
    pallas_call x1, Pallas kernels, middle(): pl.pallas_call(functools.partial(middle_kernel, sub), grid=(tokens // blo...  13.6 us
    pallas_call x1, Pallas kernels, project(): pl.pallas_call(project_kernel, grid=(tokens // block,), out_shape=(jax.Sh...  8.42 us
    pallas_call x1, Pallas kernels, input_gradient(): pl.pallas_call(input_kernel, grid=(tokens // 256,), out_shape=jax.ShapeDt...  7.33 us
    ppermute x5, starting transfers between devices, swapped(): return lax.ppermute(values, 'tensor', [(0, 1), (1, 0)])  7 us
  transfers between devices with their start and end apart: 20, of which 10 were waited for; matrix products, arithmetic and copies ran while one was open for 12% of the time, Pallas kernels for 48%

profile of v1, /device:TPU:0, one launch (start us, length us, event | category | flops | bytes accessed | tf_op | source)
XLA Modules:
  0.0 174.8 jit_solution(18008146093901278869)
XLA Ops:
  0.7 0.9 constant_dynamic-slice_fusion.4
  1.6 0.7 fusion.7
  2.4 3.0 %collective-permute-start = (bf16[400,256]{1,0:T(8,128)(2,1)S(1)}, bf16[400,256]{1,0:T(8,128)(2,1)S(1)}, u32[]{:S(2)}, u32[]{:S(2)}) collective-permute-start(bf16[400,256]{1,0:T(8,128)(2,1)S(1)} %fusion.7), channel_id=1, source_target_pairs={{0,1},{1,0},{2,3},{3,2},{4,5},{5,4},{6,7},{7,6},{8,9},{9,8},{10,11... | collective-permute-start | bytes 614408 | tf_op jit(solution)/shard_map/ppermute | solution.py:819
  5.5 0.7 compare_bitcast_fusion
  6.2 0.8 reduce-window.10
  7.0 0.7 fusion.29
  7.7 0.7 bitcast_subtract_fusion
  8.5 0.7 broadcast_compare_fusion
  10.9 0.7 fusion.10.extra_q_ref
  12.2 1.0 fusion.34
  13.2 2.0 %collective-permute-start.1 = (bf16[384,256]{1,0:T(8,128)(2,1)S(1)}, bf16[384,256]{1,0:T(8,128)(2,1)S(1)}, u32[]{:S(2)}, u32[]{:S(2)}) collective-permute-start(bf16[384,256]{1,0:T(8,128)(2,1)S(1)} %slice.209), channel_id=1, source_target_pairs={{0,4},{2,6},{4,0},{6,2},{8,12},{10,14},{12,8},{14,10},{16,20},{18,... | collective-permute-start | bytes 589832 | tf_op jit(solution)/shard_map/ppermute | solution.py:822
  15.3 4.4 %collective-permute-done.1 = bf16[384,256]{1,0:T(8,128)(2,1)S(1)} collective-permute-done((bf16[384,256]{1,0:T(8,128)(2,1)S(1)}, bf16[384,256]{1,0:T(8,128)(2,1)S(1)}, u32[]{:S(2)}, u32[]{:S(2)}) %collective-permute-start.1) | collective-permute-done | bytes 196640 | tf_op jit(solution)/shard_map/ppermute | solution.py:822
  21.0 1.2 pad_add_fusion.live_ref.refs_0_
  23.0 0.7 maximum_convert_fusion.bias_ref
  23.9 1.0 pad_maximum_fusion
  24.8 8.4 %project.1 = (bf16[8,1024,128]{2,1,0:T(8,128)(2,1)}, bf16[8,1024,128]{2,1,0:T(8,128)(2,1)}, bf16[1024,512]{1,0:T(8,128)(2,1)}, bf16[8,128,1024]{2,1,0:T(8,128)(2,1)}, bf16[1024,512]{1,0:T(8,128)(2,1)}) custom-call(bf16[1024,512]{1,0:T(8,128)(2,1)} %refs_12_.1, bf16[3,512,256]{2,1,0:T(8,128)(2,1)} %bitcast.89, bf16[3,512,256]{2,1,0:T(8,128)(2,1)} %bitcast.79, ...), custom_call_target="tpu_custom_call" | custom-call | flops 2684354560 | bytes 6291456 | tf_op jit(solution)/shard_map/project/pallas_call | solution.py:96
  33.3 1.7 collective-permute-start.4
  35.0 23.1 %attend.1 = (bf16[8,2048,1024]{2,1,0:T(8,128)(2,1)}, f32[8,64,1024]{2,1,0:T(8,128)}, f32[8,1,1024]{2,1,0:T(1,128)}, bf16[8,1024,128]{2,1,0:T(8,128)(2,1)}, bf16[...) custom-call(s32[2]{0:T(128)} %pad_add_fusion.live_ref.refs_0_, bf16[8,128,1024]{2,1,0:T(8,128)(2,1)} %get-tuple-element.52.qt_hbm, ...), custom_call_target="tpu_custom_call" | custom-call | flops 17179869184 | bytes 33554432 | tf_op jit(solution)/shard_map/attend/pallas_call | solution.py:282
  58.1 0.9 copy-done.14
  59.0 13.6 %middle.1 = (bf16[1024,512]{1,0:T(8,128)(2,1)}, f32[1024,512]{1,0:T(8,128)}, bf16[8,128,1024]{2,1,0:T(8,128)(2,1)}, bf16[1024,512]{1,0:T(8,128)(2,1)}, f32[768,5...) custom-call(bf16[1024,512]{1,0:T(8,128)(2,1)} %refs_12_.1, bf16[1024,512]{1,0:T(8,128)(2,1)} %cot_ref.1, ...), custom_call_target="tpu_custom_call" | custom-call | flops 4831838208 | bytes 10485760 | tf_op jit(solution)/shard_map/middle/pallas_call | solution.py:433
  72.7 1.0 collective-permute-start.5
  73.6 23.5 %attend_back_other.1 = (f32[512,1024]{1,0:T(8,128)}, bf16[1024,512]{1,0:T(8,128)(2,1)}, f32[2,512,512]{2,1,0:T(8,128)}, f32[2,512]{1,0:T(2,128)}) custom-call(s32[2]{0:T(128)} %pad_add_fusion.live_ref.refs_0_, s32[1,1024]{1,0:T(1,128)} %get-tuple-element.132.place_ref.refs_1_, bf16[8,2048,1024]{2,1,0:T(8,128)(2,1)} %get-tuple-element.64.refs_2_.refs_3_, ...), custom_call_target="tpu_custom_call" | custom-call | flops 17179869184 | bytes 16777216 | tf_op jit(solution)/shard_map/attend_back_other/pallas_call | solution.py:660
  97.1 1.2 collective-permute-start.7
  98.6 1.6 collective-permute-start.6
  100.2 21.7 %attend_back_own.1 = (bf16[1600,256]{1,0:T(8,128)(2,1)}, bf16[1600,256]{1,0:T(8,128)(2,1)}, bf16[1024,512]{1,0:T(8,128)(2,1)}, bf16[1024,512]{1,0:T(8,128)(2,1)}, bf16[1024,512]{1,0:T(8,128)(2,1)}) custom-call(s32[2]{0:T(128)} %pad_add_fusion.live_ref.refs_0_, f32[8,512]{1,0:T(8,128)} %get-tuple-element.74.refs_1_, f32[2,512]{1,0:T(2,128)} %get-tuple-element.75.refs_2_, ...), custom_call_target="tpu_custom_call" | custom-call | flops 17179869184 | bytes 16777216 | tf_op jit(solution)/shard_map/attend_back_own/pallas_call | solution.py:660
  121.9 0.8 collective-permute-done.7.got_ref
  122.7 1.4 bitcast_add_fusion
  124.4 1.3 collective-permute-done.15
  125.7 1.6 collective-permute-start.16
  127.4 1.3 convert_add_fusion
  128.7 0.7 subtract_convert_fusion
  129.5 0.9 collective-permute-start.9
  130.4 2.4 %collective-permute-done.16 = bf16[192,512]{1,0:T(8,128)(2,1)S(1)} collective-permute-done((bf16[192,512]{1,0:T(8,128)(2,1)S(1)}, bf16[192,512]{1,0:T(8,128)(2,1)S(1)}, u32[]{:S(2)}, u32[]{:S(2)}) %collective-permute-start.16) | collective-permute-done | bytes 196640 | tf_op jit(solution)/shard_map/ppermute | solution.py:740
  132.8 2.7 %collective-permute-start.17 = (bf16[192,512]{1,0:T(8,128)(2,1)S(1)}, bf16[192,512]{1,0:T(8,128)(2,1)S(1)}, u32[]{:S(2)}, u32[]{:S(2)}) collective-permute-start(bf16[192,512]{1,0:T(8,128)(2,1)S(1)} %add_convert_fusion.1), channel_id=1, source_target_pairs={{0,16},{2,18},{4,20},{6,22},{8,24},{10,26},{12,28},{14,30},{16,0},... | collective-permute-start | bytes 589832 | tf_op jit(solution)/shard_map/ppermute | solution.py:740
  135.5 5.3 %collective-permute-done.9 = bf16[800,256]{1,0:T(8,128)(2,1)S(1)} collective-permute-done((bf16[800,256]{1,0:T(8,128)(2,1)S(1)}, bf16[800,256]{1,0:T(8,128)(2,1)S(1)}, u32[]{:S(2)}, u32[]{:S(2)}) %collective-permute-start.9) | collective-permute-done | bytes 409632 | tf_op jit(solution)/shard_map/ppermute | solution.py:754
  140.9 0.7 fusion.16
  141.7 1.6 collective-permute-start.10
  143.2 0.9 collective-permute-done.17
  144.3 3.7 %collective-permute-done.10 = bf16[416,256]{1,0:T(8,128)(2,1)S(1)} collective-permute-done((bf16[416,256]{1,0:T(8,128)(2,1)S(1)}, bf16[416,256]{1,0:T(8,128)(2,1)S(1)}, u32[]{:S(2)}, u32[]{:S(2)}) %collective-permute-start.10) | collective-permute-done | bytes 213024 | tf_op jit(solution)/shard_map/ppermute | solution.py:740
  148.7 1.6 collective-permute-start.19
  150.2 3.8 %collective-permute-done.11 = bf16[416,256]{1,0:T(8,128)(2,1)S(1)} collective-permute-done((bf16[416,256]{1,0:T(8,128)(2,1)S(1)}, bf16[416,256]{1,0:T(8,128)(2,1)S(1)}, u32[]{:S(2)}, u32[]{:S(2)}) %collective-permute-start.11) | collective-permute-done | bytes 213024 | tf_op jit(solution)/shard_map/ppermute | solution.py:740
  154.1 4.2 %collective-permute-start.12 = (bf16[416,256]{1,0:T(8,128)(2,1)S(1)}, bf16[416,256]{1,0:T(8,128)(2,1)S(1)}, u32[]{:S(2)}, u32[]{:S(2)}) collective-permute-start(bf16[416,256]{1,0:T(8,128)(2,1)S(1)} %pad_maximum_fusion.10), channel_id=1, source_target_pairs={{0,16},{2,18},{4,20},{6,22},{8,24},{10,26},{12,28},{14,30},{16,0},... | collective-permute-start | bytes 638984 | tf_op jit(solution)/shard_map/ppermute | solution.py:740
  158.3 7.3 %input_gradient.1 = f32[1024,512]{1,0:T(8,128)} custom-call(f32[1024,512]{1,0:T(8,128)} %get-tuple-element.61.res_ref, bf16[1024,512]{1,0:T(8,128)(2,1)} %copy-done.1, bf16[1024,512]{1,0:T(8,128)(2,1)} %get-tuple-element.83.dq_ref, bf16[1024,512]{1,0:T(8,128)(2,1)} %get-tuple-element.84.dk_ref, bf16[1024,512]{1,0:T(8,128)(2,1)} %get-tuple-element.85.dv_ref, ...), custom_call_target="tpu_custom_call" | custom-call | flops 1610612736 | bytes 8388608 | tf_op jit(solution)/shard_map/input_gradient/pallas_call | solution.py:699
  165.7 1.5 collective-permute-start.13
  167.3 1.2 fusion.6
  169.7 1.8 %collective-permute-done.13 = bf16[384,256]{1,0:T(8,128)(2,1)S(1)} collective-permute-done((bf16[384,256]{1,0:T(8,128)(2,1)S(1)}, bf16[384,256]{1,0:T(8,128)(2,1)S(1)}, u32[]{:S(2)}, u32[]{:S(2)}) %collective-permute-start.13) | collective-permute-done | bytes 196640 | tf_op jit(solution)/shard_map/ppermute | solution.py:740
  172.3 0.8 pad_maximum_fusion.2
  173.5 1.3 convert_bitcast_fusion
  (113 shorter events, 9.2 us)
Async XLA Ops:
  2.3 19.9 %copy-start.15 = (bf16[256]{0:T(256)(128)(2,1)S(1)}, bf16[256]{0:T(256)(128)(2,1)}, u32[]{:S(2)}) copy-start(bf16[256]{0:T(256)(128)(2,1)} %param.26) | copy-start | bytes 1540
  2.3 19.9 %copy-start.6 = (f32[512]{0:T(512)S(1)}, f32[512]{0:T(512)}, u32[]{:S(2)}) copy-start(f32[512]{0:T(512)} %param.22) | copy-start | bytes 6148
  2.3 19.9 %copy-start.8 = (f32[512]{0:T(512)S(1)}, f32[512]{0:T(512)}, u32[]{:S(2)}) copy-start(f32[512]{0:T(512)} %param.23) | copy-start | bytes 6148
  2.4 19.9 %copy-start.9 = (f32[512]{0:T(512)S(1)}, f32[512]{0:T(512)}, u32[]{:S(2)}) copy-start(f32[512]{0:T(512)} %param.24) | copy-start | bytes 6148
  2.4 19.9 %copy-start.10 = (f32[512]{0:T(512)S(1)}, f32[512]{0:T(512)}, u32[]{:S(2)}) copy-start(f32[512]{0:T(512)} %param.28) | copy-start | bytes 6148
  2.4 19.9 %copy-start.11 = (f32[512]{0:T(512)S(1)}, f32[512]{0:T(512)}, u32[]{:S(2)}) copy-start(f32[512]{0:T(512)} %param.29) | copy-start | bytes 6148
  2.4 19.9 %copy-start.12 = (f32[512]{0:T(512)S(1)}, f32[512]{0:T(512)}, u32[]{:S(2)}) copy-start(f32[512]{0:T(512)} %param.30) | copy-start | bytes 6148
  2.4 20.5 %copy-start.4 = (bf16[256,512]{1,0:T(8,128)(2,1)S(1)}, bf16[256,512]{1,0:T(8,128)(2,1)}, u32[]{:S(2)}) copy-start(bf16[256,512]{1,0:T(8,128)(2,1)} %param.27) | copy-start | bytes 786436
  2.4 20.5 %copy-start.5 = (bf16[256,512]{1,0:T(8,128)(2,1)S(1)}, bf16[256,512]{1,0:T(8,128)(2,1)}, u32[]{:S(2)}) copy-start(bf16[256,512]{1,0:T(8,128)(2,1)} %param.21) | copy-start | bytes 786436
  2.4 10.8 %collective-permute-start = (bf16[400,256]{1,0:T(8,128)(2,1)S(1)}, bf16[400,256]{1,0:T(8,128)(2,1)S(1)}, u32[]{:S(2)}, u32[]{:S(2)}) collective-permute-start(bf16[400,256]{1,0:T(8,128)(2,1)S(1)} %fusion.7), channel_id=1, source_target_pairs={{0,1},{1,0},{2,3},{3,2},{4,5},{5,4},{6,7},{7,6},{8,9},{9,8},{10,11... | collective-permute-start | bytes 614408 | tf_op jit(solution)/shard_map/ppermute | solution.py:819
  5.5 27.8 %collective-permute-start.3 = (bf16[1024,512]{1,0:T(8,128)(2,1)}, bf16[1024,512]{1,0:T(8,128)(2,1)S(1)}, u32[]{:S(2)}, u32[]{:S(2)}) collective-permute-start(bf16[1024,512]{1,0:T(8,128)(2,1)} %refs_12_.1), channel_id=1, source_target_pairs={{0,1},{1,0},{2,3},{3,2},{4,5},{5,4},{6,7},{7,6},{8,9},{9,8},{10,11... | collective-permute-start | bytes 3145736 | tf_op jit(solution)/shard_map/ppermute | solution.py:819
  13.2 6.4 %collective-permute-start.1 = (bf16[384,256]{1,0:T(8,128)(2,1)S(1)}, bf16[384,256]{1,0:T(8,128)(2,1)S(1)}, u32[]{:S(2)}, u32[]{:S(2)}) collective-permute-start(bf16[384,256]{1,0:T(8,128)(2,1)S(1)} %slice.209), channel_id=1, source_target_pairs={{0,4},{2,6},{4,0},{6,2},{8,12},{10,14},{12,8},{14,10},{16,20},{18,... | collective-permute-start | bytes 589832 | tf_op jit(solution)/shard_map/ppermute | solution.py:822
  15.3 7.7 %copy-start.7 = (bf16[2,256]{1,0:T(2,128)(2,1)S(1)}, bf16[2,256]{1,0:T(2,128)(2,1)}, u32[]{:S(2)}) copy-start(bf16[2,256]{1,0:T(2,128)(2,1)} %param.20) | copy-start | bytes 3076
  19.7 4.0 %collective-permute-start.2 = (bf16[768,256]{1,0:T(8,128)(2,1)S(1)}, bf16[768,256]{1,0:T(8,128)(2,1)S(1)}, u32[]{:S(2)}, u32[]{:S(2)}) collective-permute-start(bf16[768,256]{1,0:T(8,128)(2,1)S(1)} %pad_maximum_fusion.4), channel_id=1, source_target_pairs={{0,2},{2,0},{4,6},{6,4},{8,10},{10,8},{12,14},{14,12},{16,18},{18,... | collective-permute-start | bytes 1179656 | tf_op jit(solution)/shard_map/ppermute | solution.py:822
  23.0 10.3 %copy-start.3 = (bf16[784,512]{1,0:T(8,128)(2,1)}, bf16[784,512]{1,0:T(8,128)(2,1)S(1)}, u32[]{:S(2)}) copy-start(bf16[784,512]{1,0:T(8,128)(2,1)S(1)} %fusion.1.w_own_ref) | copy-start | bytes 2408452
  33.3 1.8 %copy-start.13 = (bf16[1024,512]{1,0:T(8,128)(2,1)}, bf16[1024,512]{1,0:T(8,128)(2,1)S(1)}, u32[]{:S(2)}) copy-start(bf16[1024,512]{1,0:T(8,128)(2,1)S(1)} %collective-permute-done.3.x_ref) | copy-start | bytes 3145732
  33.3 24.8 %collective-permute-start.4 = (bf16[784,512]{1,0:T(8,128)(2,1)S(1)}, bf16[784,512]{1,0:T(8,128)(2,1)S(1)}, u32[]{:S(2)}, u32[]{:S(2)}) collective-permute-start(bf16[784,512]{1,0:T(8,128)(2,1)S(1)} %fusion.1.w_own_ref), channel_id=1, source_target_pairs={{0,1},{1,0},{2,3},{3,2},{4,5},{5,4},{6,7},{7,6},{8,9},{9,8},{10,11... | collective-permute-start | bytes 2408456 | tf_op jit(solution)/shard_map/ppermute | solution.py:819
  58.1 0.9 copy-start.14
  72.7 25.7 %collective-permute-start.5 = (bf16[768,512]{1,0:T(8,128)(2,1)}, bf16[768,512]{1,0:T(8,128)(2,1)S(1)}, u32[]{:S(2)}, u32[]{:S(2)}) collective-permute-start(bf16[768,512]{1,0:T(8,128)(2,1)} %get-tuple-element.63), channel_id=1, source_target_pairs={{0,1},{1,0},{2,3},{3,2},{4,5},{5,4},{6,7},{7,6},{8,9},{9,8},{10,11... | collective-permute-start | bytes 2359304 | tf_op jit(solution)/shard_map/ppermute | solution.py:819
  73.6 24.7 %copy-start = (f32[768,512]{1,0:T(8,128)S(1)}, f32[768,512]{1,0:T(8,128)}, u32[]{:S(2)}) copy-start(f32[768,512]{1,0:T(8,128)} %get-tuple-element.62) | copy-start | bytes 4718596
  97.1 25.5 %collective-permute-start.7 = (bf16[1024,512]{1,0:T(8,128)(2,1)}, bf16[1024,512]{1,0:T(8,128)(2,1)S(1)}, u32[]{:S(2)}, u32[]{:S(2)}) collective-permute-start(bf16[1024,512]{1,0:T(8,128)(2,1)} %get-tuple-element.73), channel_id=1, source_target_pairs={{0,1},{1,0},{2,3},{3,2},{4,5},{5,4},{6,7},{7,6},{8,9},{9,8},{10,11... | collective-permute-start | bytes 3145736 | tf_op jit(solution)/shard_map/ppermute | solution.py:819
  98.6 24.0 %collective-permute-start.6 = (bf16[384,512]{1,0:T(8,128)(2,1)S(1)}, bf16[384,512]{1,0:T(8,128)(2,1)}, u32[]{:S(2)}, u32[]{:S(2)}) collective-permute-start(bf16[384,512]{1,0:T(8,128)(2,1)S(1)} %fusion.3), channel_id=1, source_target_pairs={{0,4},{2,6},{4,0},{6,2},{8,12},{10,14},{12,8},{14,10},{16,20},{18,... | collective-permute-start | bytes 1179656 | tf_op jit(solution)/shard_map/ppermute | solution.py:822
  122.7 6.0 %copy-start.1 = (bf16[1024,512]{1,0:T(8,128)(2,1)}, bf16[1024,512]{1,0:T(8,128)(2,1)S(1)}, u32[]{:S(2)}) copy-start(bf16[1024,512]{1,0:T(8,128)(2,1)S(1)} %collective-permute-done.7.got_ref) | copy-start | bytes 3145732
  122.7 4.7 %collective-permute-start.8 = (bf16[1600,256]{1,0:T(8,128)(2,1)}, bf16[1600,256]{1,0:T(8,128)(2,1)}, u32[]{:S(2)}, u32[]{:S(2)}) collective-permute-start(bf16[1600,256]{1,0:T(8,128)(2,1)} %get-tuple-element.82), channel_id=1, source_target_pairs={{0,2},{2,0},{4,6},{6,4},{8,10},{10,8},{12,14},{14,12},{16,18},{18,... | collective-permute-start | bytes 2457608 | tf_op jit(solution)/shard_map/ppermute | solution.py:740
  124.1 3.3 %copy-start.2 = (bf16[1600,256]{1,0:T(8,128)(2,1)S(1)}, bf16[1600,256]{1,0:T(8,128)(2,1)}, u32[]{:S(2)}) copy-start(bf16[1600,256]{1,0:T(8,128)(2,1)} %get-tuple-element.86) | copy-start | bytes 2457604
  124.1 1.5 collective-permute-start.15
  125.7 7.1 %collective-permute-start.16 = (bf16[192,512]{1,0:T(8,128)(2,1)S(1)}, bf16[192,512]{1,0:T(8,128)(2,1)S(1)}, u32[]{:S(2)}, u32[]{:S(2)}) collective-permute-start(bf16[192,512]{1,0:T(8,128)(2,1)S(1)} %fusion.4), channel_id=1, source_target_pairs={{0,8},{2,10},{4,12},{6,14},{8,0},{10,2},{12,4},{14,6},{16,24},{18,... | collective-permute-start | bytes 589832 | tf_op jit(solution)/shard_map/ppermute | solution.py:740
  129.5 11.3 %collective-permute-start.9 = (bf16[800,256]{1,0:T(8,128)(2,1)S(1)}, bf16[800,256]{1,0:T(8,128)(2,1)S(1)}, u32[]{:S(2)}, u32[]{:S(2)}) collective-permute-start(bf16[800,256]{1,0:T(8,128)(2,1)S(1)} %pad_maximum_fusion.3), channel_id=1, source_target_pairs={{0,1},{1,0},{2,3},{3,2},{4,5},{5,4},{6,7},{7,6},{8,9},{9,8},{10,11... | collective-permute-start | bytes 1228808 | tf_op jit(solution)/shard_map/ppermute | solution.py:754
  132.8 11.3 %collective-permute-start.17 = (bf16[192,512]{1,0:T(8,128)(2,1)S(1)}, bf16[192,512]{1,0:T(8,128)(2,1)S(1)}, u32[]{:S(2)}, u32[]{:S(2)}) collective-permute-start(bf16[192,512]{1,0:T(8,128)(2,1)S(1)} %add_convert_fusion.1), channel_id=1, source_target_pairs={{0,16},{2,18},{4,20},{6,22},{8,24},{10,26},{12,28},{14,30},{16,0},... | collective-permute-start | bytes 589832 | tf_op jit(solution)/shard_map/ppermute | solution.py:740
  141.7 6.3 %collective-permute-start.10 = (bf16[416,256]{1,0:T(8,128)(2,1)S(1)}, bf16[416,256]{1,0:T(8,128)(2,1)S(1)}, u32[]{:S(2)}, u32[]{:S(2)}) collective-permute-start(bf16[416,256]{1,0:T(8,128)(2,1)S(1)} %pad_maximum_fusion.8), channel_id=1, source_target_pairs={{0,4},{2,6},{4,0},{6,2},{8,12},{10,14},{12,8},{14,10},{16,20},{18,... | collective-permute-start | bytes 638984 | tf_op jit(solution)/shard_map/ppermute | solution.py:740
  144.2 4.4 %collective-permute-start.18 = (bf16[192,512]{1,0:T(8,128)(2,1)S(1)}, bf16[192,512]{1,0:T(8,128)(2,1)S(1)}, u32[]{:S(2)}, u32[]{:S(2)}) collective-permute-start(bf16[192,512]{1,0:T(8,128)(2,1)S(1)} %add_convert_fusion), channel_id=1, source_target_pairs={{0,2},{2,0},{4,6},{6,4},{8,10},{10,8},{12,14},{14,12},{16,18},{18,... | collective-permute-start | bytes 589832 | tf_op jit(solution)/shard_map/ppermute | solution.py:740
  148.1 5.9 %collective-permute-start.11 = (bf16[416,256]{1,0:T(8,128)(2,1)S(1)}, bf16[416,256]{1,0:T(8,128)(2,1)S(1)}, u32[]{:S(2)}, u32[]{:S(2)}) collective-permute-start(bf16[416,256]{1,0:T(8,128)(2,1)S(1)} %pad_maximum_fusion.9), channel_id=1, source_target_pairs={{0,8},{2,10},{4,12},{6,14},{8,0},{10,2},{12,4},{14,6},{16,24},{18,... | collective-permute-start | bytes 638984 | tf_op jit(solution)/shard_map/ppermute | solution.py:740
  148.7 17.0 %collective-permute-start.19 = (bf16[384,512]{1,0:T(8,128)(2,1)S(1)}, bf16[384,512]{1,0:T(8,128)(2,1)S(1)}, u32[]{:S(2)}, u32[]{:S(2)}) collective-permute-start(bf16[384,512]{1,0:T(8,128)(2,1)S(1)} %pad_maximum_fusion.6), channel_id=1, source_target_pairs={{0,4},{2,6},{4,0},{6,2},{8,12},{10,14},{12,8},{14,10},{16,20},{18,... | collective-permute-start | bytes 1179656 | tf_op jit(solution)/shard_map/ppermute | solution.py:740
  154.1 11.6 %collective-permute-start.12 = (bf16[416,256]{1,0:T(8,128)(2,1)S(1)}, bf16[416,256]{1,0:T(8,128)(2,1)S(1)}, u32[]{:S(2)}, u32[]{:S(2)}) collective-permute-start(bf16[416,256]{1,0:T(8,128)(2,1)S(1)} %pad_maximum_fusion.10), channel_id=1, source_target_pairs={{0,16},{2,18},{4,20},{6,22},{8,24},{10,26},{12,28},{14,30},{16,0},... | collective-permute-start | bytes 638984 | tf_op jit(solution)/shard_map/ppermute | solution.py:740
  165.7 5.7 %collective-permute-start.13 = (bf16[384,256]{1,0:T(8,128)(2,1)S(1)}, bf16[384,256]{1,0:T(8,128)(2,1)S(1)}, u32[]{:S(2)}, u32[]{:S(2)}) collective-permute-start(bf16[384,256]{1,0:T(8,128)(2,1)S(1)} %add_convert_fusion.2), channel_id=1, source_target_pairs={{0,4},{2,6},{4,0},{6,2},{8,12},{10,14},{12,8},{14,10},{16,20},{18,... | collective-permute-start | bytes 589832 | tf_op jit(solution)/shard_map/ppermute | solution.py:740
  171.5 1.8 %collective-permute-start.14 = (bf16[768,256]{1,0:T(8,128)(2,1)S(1)}, bf16[768,256]{1,0:T(8,128)(2,1)S(1)}, u32[]{:S(2)}, u32[]{:S(2)}) collective-permute-start(bf16[768,256]{1,0:T(8,128)(2,1)S(1)} %pad_maximum_fusion.5), channel_id=1, source_target_pairs={{0,2},{2,0},{4,6},{6,4},{8,10},{10,8},{12,14},{14,12},{16,18},{18,... | collective-permute-start | bytes 1179656 | tf_op jit(solution)/shard_map/ppermute | solution.py:740

commit v2 on v1

--- a/solution.py
+++ b/solution.py
@@ -464,10 +464,10 @@
 
 def backward_kernel(sub, part, *refs):
     if part:
-        (live_ref, place_ref, p_hbm, dot_hbm, dnat_hbm, q_hbm, k_hbm, v_hbm, x_hbm, own_hbm, oth_hbm,
+        (live_ref, p_hbm, dot_hbm, dnat_hbm, q_hbm, k_hbm, v_hbm, x_hbm, own_hbm, oth_hbm,
          dq_hbm, dx_ref, gw_ref, bias_ref,
          dot_ref, dnat_ref, q_ref, k_ref, v_ref, x_ref, own_ref, oth_ref,
-         dq_ref, dk_ref, dv_ref, dx_scr, acc_scr, p_scr, sem, pair_sem, last_sem, out_sem) = refs
+         dq_ref, dk_ref, dv_ref, acc_scr, p_scr, sem, pair_sem, last_sem, out_sem) = refs
         more = ((own_hbm, own_ref), (oth_hbm, oth_ref))
     else:
         (live_ref, small_ref, value_ref,
@@ -602,11 +602,7 @@
             rows = pl.ds(pl.multiple_of(i * sub, sub), sub)
             dk, dv = dk_ref[rows, :], dv_ref[rows, :]
             dx = times_weights(dk, own_ref, oth_ref, 1) + times_weights(dv, own_ref, oth_ref, 2)
-            dx_scr[rows, :] = dx.astype(BF)
-
-        for at in range(0, keys, sub):
-            rows, earlier = slice(at, at + sub), at + sub
-            dx_ref[rows, :] = dot(live_rows(place_ref, 0, earlier, rows), dx_scr[:earlier, :], 0, 0).astype(BF)
+            dx_ref[rows, :] = dx.astype(BF)
     else:
         dq_out[...] = ((before_ref[...] + dq_ref[...]) * HD**-0.5).astype(BF).T
         gq_ref[...] = dot(whole_ref[...], dq_out[...], 0, 0)
@@ -650,7 +646,6 @@
     if part:
         out_shape = (turned, grad, sums, jax.ShapeDtypeStruct((2, width), F32))
         out_specs = (HBM, VMEM, VMEM, VMEM)
-        held.append(pltpu.VMEM(grad.shape, BF))
     else:
         payload = jax.ShapeDtypeStruct((3 * width + 64, width // 2), BF)
         out_shape = (payload, payload, grad, grad, grad)
@@ -686,9 +681,11 @@
         live_scr[...] = jnp.zeros_like(live_scr)
 
     live_scr[pl.ds(pl.multiple_of(step * block, block), block), :] = (
-        times_weights(dk_ref[...], own_ref, oth_ref, 1) + times_weights(dv_ref[...], own_ref, oth_ref, 2)
+        times_weights(dk_ref[...], own_ref, oth_ref, 1)
+        + times_weights(dv_ref[...], own_ref, oth_ref, 2)
+        + got_ref[...].astype(F32)
     ).astype(BF)
-    dx = res_ref[...] + got_ref[...].astype(F32) + times_weights(dq_ref[...], own_ref, oth_ref, 0)
+    dx = res_ref[...] + times_weights(dq_ref[...], own_ref, oth_ref, 0)
     dx_ref[...] = dx + dot(live_rows(place_ref, 0, live_scr.shape[0]), live_scr[...], 0, 0)
 
 
@@ -850,7 +847,7 @@
     )
     mid_got = swapped(mid_oth)
     dq, dx_oth, sums, value_grad = attend_backward(
-        1, (live, place_oth), probs, dot_turned, dnat, q, k_oth, v_oth, x_oth, w_own, w_oth
+        1, (live,), probs, dot_turned, dnat, q, k_oth, v_oth, x_oth, w_own, w_oth
     )
     mid_got, dq = lax.optimization_barrier((mid_got, dq))
     mid = (mid_own + mid_got.astype(F32)).reshape(2, 3 * shard // 2, width)

time: 175 us -> 175 us (level)
  no operation moved by 1% of the time
where the time goes in v2:
time: 175 us; the launch traced here: 174 us
  Pallas kernels  96.9 us (55%)
  starting transfers between devices  25.6 us (15%)
  waiting for transfers between devices  24.3 us (14%)
  other arithmetic  19.6 us (11%)
  local copies, waits for them, and re-layouts  6.22 us (4%)
    pallas_call x2, Pallas kernels, attend_backward(): pl.pallas_call(functools.partial(backward_kernel, sub, part), out_shape=o...  44.5 us
    pallas_call x1, Pallas kernels, attend(): pl.pallas_call(functools.partial(attend_kernel, count, chunk), out_shape=...  23.1 us
    ppermute x14, waiting for transfers between devices, across(): return lax.ppermute(values, 'dp', [(i, i ^ bit) for i in range(devices)])  18.3 us
    ppermute x14, starting transfers between devices, across(): return lax.ppermute(values, 'dp', [(i, i ^ bit) for i in range(devices)])  17.7 us
    pallas_call x1, Pallas kernels, middle(): pl.pallas_call(functools.partial(middle_kernel, sub), grid=(tokens // blo...  13.6 us
    pallas_call x1, Pallas kernels, project(): pl.pallas_call(project_kernel, grid=(tokens // block,), out_shape=(jax.Sh...  8.41 us
    pallas_call x1, Pallas kernels, input_gradient(): pl.pallas_call(input_kernel, grid=(tokens // 256,), out_shape=jax.ShapeDt...  7.34 us
    ppermute x5, starting transfers between devices, swapped(): return lax.ppermute(values, 'tensor', [(0, 1), (1, 0)])  7.01 us
  transfers between devices with their start and end apart: 20, of which 10 were waited for; matrix products, arithmetic and copies ran while one was open for 12% of the time, Pallas kernels for 48%

profile of v2, /device:TPU:0, one launch (start us, length us, event | category | flops | bytes accessed | tf_op | source)
XLA Modules:
  0.0 173.9 jit_solution(4877027769986138391)
XLA Ops:
  0.7 0.9 constant_dynamic-slice_fusion.4
  1.6 0.7 fusion.7
  2.4 3.0 %collective-permute-start = (bf16[400,256]{1,0:T(8,128)(2,1)S(1)}, bf16[400,256]{1,0:T(8,128)(2,1)S(1)}, u32[]{:S(2)}, u32[]{:S(2)}) collective-permute-start(bf16[400,256]{1,0:T(8,128)(2,1)S(1)} %fusion.7), channel_id=1, source_target_pairs={{0,1},{1,0},{2,3},{3,2},{4,5},{5,4},{6,7},{7,6},{8,9},{9,8},{10,11... | collective-permute-start | bytes 614408 | tf_op jit(solution)/shard_map/ppermute | solution.py:816
  5.5 0.7 compare_bitcast_fusion
  6.2 0.8 reduce-window.10
  7.0 0.7 fusion.29
  7.7 0.7 bitcast_subtract_fusion
  8.5 0.7 broadcast_compare_fusion
  10.9 0.7 fusion.10.extra_q_ref
  12.2 1.0 fusion.34
  13.2 2.0 %collective-permute-start.1 = (bf16[384,256]{1,0:T(8,128)(2,1)S(1)}, bf16[384,256]{1,0:T(8,128)(2,1)S(1)}, u32[]{:S(2)}, u32[]{:S(2)}) collective-permute-start(bf16[384,256]{1,0:T(8,128)(2,1)S(1)} %slice.209), channel_id=1, source_target_pairs={{0,4},{2,6},{4,0},{6,2},{8,12},{10,14},{12,8},{14,10},{16,20},{18,... | collective-permute-start | bytes 589832 | tf_op jit(solution)/shard_map/ppermute | solution.py:819
  15.3 4.4 %collective-permute-done.1 = bf16[384,256]{1,0:T(8,128)(2,1)S(1)} collective-permute-done((bf16[384,256]{1,0:T(8,128)(2,1)S(1)}, bf16[384,256]{1,0:T(8,128)(2,1)S(1)}, u32[]{:S(2)}, u32[]{:S(2)}) %collective-permute-start.1) | collective-permute-done | bytes 196640 | tf_op jit(solution)/shard_map/ppermute | solution.py:819
  21.0 1.2 pad_add_fusion.live_ref.refs_0_
  22.3 0.6 stack.56.vec_ref
  23.0 0.7 maximum_convert_fusion.bias_ref
  23.9 1.0 pad_maximum_fusion
  24.8 8.4 %project.1 = (bf16[8,1024,128]{2,1,0:T(8,128)(2,1)}, bf16[8,1024,128]{2,1,0:T(8,128)(2,1)}, bf16[1024,512]{1,0:T(8,128)(2,1)}, bf16[8,128,1024]{2,1,0:T(8,128)(2,1)}, bf16[1024,512]{1,0:T(8,128)(2,1)}) custom-call(bf16[1024,512]{1,0:T(8,128)(2,1)} %refs_12_.1, bf16[3,512,256]{2,1,0:T(8,128)(2,1)} %bitcast.89, bf16[3,512,256]{2,1,0:T(8,128)(2,1)} %bitcast.79, ...), custom_call_target="tpu_custom_call" | custom-call | flops 2684354560 | bytes 6291456 | tf_op jit(solution)/shard_map/project/pallas_call | solution.py:96
  33.3 1.7 %collective-permute-start.4 = (bf16[784,512]{1,0:T(8,128)(2,1)S(1)}, bf16[784,512]{1,0:T(8,128)(2,1)S(1)}, u32[]{:S(2)}, u32[]{:S(2)}) collective-permute-start(bf16[784,512]{1,0:T(8,128)(2,1)S(1)} %fusion.1.w_own_ref), channel_id=1, source_target_pairs={{0,1},{1,0},{2,3},{3,2},{4,5},{5,4},{6,7},{7,6},{8,9},{9,8},{10,11... | collective-permute-start | bytes 2408456 | tf_op jit(solution)/shard_map/ppermute | solution.py:816
  35.0 23.1 %attend.1 = (bf16[8,2048,1024]{2,1,0:T(8,128)(2,1)}, f32[8,64,1024]{2,1,0:T(8,128)}, f32[8,1,1024]{2,1,0:T(1,128)}, bf16[8,1024,128]{2,1,0:T(8,128)(2,1)}, bf16[...) custom-call(s32[2]{0:T(128)} %pad_add_fusion.live_ref.refs_0_, bf16[8,128,1024]{2,1,0:T(8,128)(2,1)} %get-tuple-element.52.qt_hbm, ...), custom_call_target="tpu_custom_call" | custom-call | flops 17179869184 | bytes 33554432 | tf_op jit(solution)/shard_map/attend/pallas_call | solution.py:282
  58.1 0.9 copy-done.14
  59.0 13.6 %middle.1 = (bf16[1024,512]{1,0:T(8,128)(2,1)}, f32[1024,512]{1,0:T(8,128)}, bf16[8,128,1024]{2,1,0:T(8,128)(2,1)}, bf16[1024,512]{1,0:T(8,128)(2,1)}, f32[768,5...) custom-call(bf16[1024,512]{1,0:T(8,128)(2,1)} %refs_12_.1, bf16[1024,512]{1,0:T(8,128)(2,1)} %cot_ref.1, ...), custom_call_target="tpu_custom_call" | custom-call | flops 4831838208 | bytes 10485760 | tf_op jit(solution)/shard_map/middle/pallas_call | solution.py:433
  72.7 0.9 collective-permute-start.5
  73.6 22.6 %attend_back_other.1 = (f32[512,1024]{1,0:T(8,128)}, bf16[1024,512]{1,0:T(8,128)(2,1)}, f32[2,512,512]{2,1,0:T(8,128)}, f32[2,512]{1,0:T(2,128)}) custom-call(s32[2]{0:T(128)} %pad_add_fusion.live_ref.refs_0_, bf16[8,2048,1024]{2,1,0:T(8,128)(2,1)} %get-tuple-element.64.refs_1_.refs_3_, bf16[8,128,1024]{2,1,0:T(8,128)(2,1)} %get-tuple-element.65.refs_2_.refs_4_, ...), custom_call_target="tpu_custom_call" | custom-call | flops 17179869184 | bytes 16777216 | tf_op jit(solution)/shard_map/attend_back_other/pallas_call | solution.py:655
  96.2 1.2 collective-permute-start.7
  97.8 1.5 collective-permute-start.6
  99.3 21.8 %attend_back_own.1 = (bf16[1600,256]{1,0:T(8,128)(2,1)}, bf16[1600,256]{1,0:T(8,128)(2,1)}, bf16[1024,512]{1,0:T(8,128)(2,1)}, bf16[1024,512]{1,0:T(8,128)(2,1)}, bf16[1024,512]{1,0:T(8,128)(2,1)}) custom-call(s32[2]{0:T(128)} %pad_add_fusion.live_ref.refs_0_, f32[8,512]{1,0:T(8,128)} %get-tuple-element.74.refs_1_, f32[2,512]{1,0:T(2,128)} %get-tuple-element.75.refs_2_, ...), custom_call_target="tpu_custom_call" | custom-call | flops 17179869184 | bytes 16777216 | tf_op jit(solution)/shard_map/attend_back_own/pallas_call | solution.py:655
  121.8 1.4 bitcast_add_fusion
  123.5 1.3 collective-permute-done.15
  124.8 1.6 collective-permute-start.16
  126.5 1.3 convert_add_fusion
  127.8 0.7 subtract_convert_fusion
  128.6 0.9 collective-permute-start.9
  129.5 2.4 %collective-permute-done.16 = bf16[192,512]{1,0:T(8,128)(2,1)S(1)} collective-permute-done((bf16[192,512]{1,0:T(8,128)(2,1)S(1)}, bf16[192,512]{1,0:T(8,128)(2,1)S(1)}, u32[]{:S(2)}, u32[]{:S(2)}) %collective-permute-start.16) | collective-permute-done | bytes 196640 | tf_op jit(solution)/shard_map/ppermute | solution.py:737
  131.9 2.7 %collective-permute-start.17 = (bf16[192,512]{1,0:T(8,128)(2,1)S(1)}, bf16[192,512]{1,0:T(8,128)(2,1)S(1)}, u32[]{:S(2)}, u32[]{:S(2)}) collective-permute-start(bf16[192,512]{1,0:T(8,128)(2,1)S(1)} %add_convert_fusion.1), channel_id=1, source_target_pairs={{0,16},{2,18},{4,20},{6,22},{8,24},{10,26},{12,28},{14,30},{16,0},... | collective-permute-start | bytes 589832 | tf_op jit(solution)/shard_map/ppermute | solution.py:737
  134.6 5.3 %collective-permute-done.9 = bf16[800,256]{1,0:T(8,128)(2,1)S(1)} collective-permute-done((bf16[800,256]{1,0:T(8,128)(2,1)S(1)}, bf16[800,256]{1,0:T(8,128)(2,1)S(1)}, u32[]{:S(2)}, u32[]{:S(2)}) %collective-permute-start.9) | collective-permute-done | bytes 409632 | tf_op jit(solution)/shard_map/ppermute | solution.py:751
  140.0 0.7 fusion.16
  140.8 1.6 collective-permute-start.10
  142.4 0.9 collective-permute-done.17
  143.4 3.7 %collective-permute-done.10 = bf16[416,256]{1,0:T(8,128)(2,1)S(1)} collective-permute-done((bf16[416,256]{1,0:T(8,128)(2,1)S(1)}, bf16[416,256]{1,0:T(8,128)(2,1)S(1)}, u32[]{:S(2)}, u32[]{:S(2)}) %collective-permute-start.10) | collective-permute-done | bytes 213024 | tf_op jit(solution)/shard_map/ppermute | solution.py:737
  147.8 1.6 collective-permute-start.19
  149.4 3.7 %collective-permute-done.11 = bf16[416,256]{1,0:T(8,128)(2,1)S(1)} collective-permute-done((bf16[416,256]{1,0:T(8,128)(2,1)S(1)}, bf16[416,256]{1,0:T(8,128)(2,1)S(1)}, u32[]{:S(2)}, u32[]{:S(2)}) %collective-permute-start.11) | collective-permute-done | bytes 213024 | tf_op jit(solution)/shard_map/ppermute | solution.py:737
  153.2 4.2 %collective-permute-start.12 = (bf16[416,256]{1,0:T(8,128)(2,1)S(1)}, bf16[416,256]{1,0:T(8,128)(2,1)S(1)}, u32[]{:S(2)}, u32[]{:S(2)}) collective-permute-start(bf16[416,256]{1,0:T(8,128)(2,1)S(1)} %pad_maximum_fusion.10), channel_id=1, source_target_pairs={{0,16},{2,18},{4,20},{6,22},{8,24},{10,26},{12,28},{14,30},{16,0},... | collective-permute-start | bytes 638984 | tf_op jit(solution)/shard_map/ppermute | solution.py:737
  157.4 7.3 %input_gradient.1 = f32[1024,512]{1,0:T(8,128)} custom-call(f32[1024,512]{1,0:T(8,128)} %get-tuple-element.61.res_ref, bf16[1024,512]{1,0:T(8,128)(2,1)} %copy-done.1, bf16[1024,512]{1,0:T(8,128)(2,1)} %get-tuple-element.83.dq_ref, bf16[1024,512]{1,0:T(8,128)(2,1)} %get-tuple-element.84.dk_ref, bf16[1024,512]{1,0:T(8,128)(2,1)} %get-tuple-element.85.dv_ref, ...), custom_call_target="tpu_custom_call" | custom-call | flops 1610612736 | bytes 8388608 | tf_op jit(solution)/shard_map/input_gradient/pallas_call | solution.py:696
  164.8 1.5 collective-permute-start.13
  166.4 1.2 fusion.6
  168.8 1.8 %collective-permute-done.13 = bf16[384,256]{1,0:T(8,128)(2,1)S(1)} collective-permute-done((bf16[384,256]{1,0:T(8,128)(2,1)S(1)}, bf16[384,256]{1,0:T(8,128)(2,1)S(1)}, u32[]{:S(2)}, u32[]{:S(2)}) %collective-permute-start.13) | collective-permute-done | bytes 196640 | tf_op jit(solution)/shard_map/ppermute | solution.py:737
  171.3 0.8 pad_maximum_fusion.2
  172.6 1.3 convert_bitcast_fusion
  (113 shorter events, 9.2 us)
Async XLA Ops:
  2.3 19.9 %copy-start.15 = (bf16[256]{0:T(256)(128)(2,1)S(1)}, bf16[256]{0:T(256)(128)(2,1)}, u32[]{:S(2)}) copy-start(bf16[256]{0:T(256)(128)(2,1)} %param.26) | copy-start | bytes 1540
  2.3 19.9 %copy-start.6 = (f32[512]{0:T(512)S(1)}, f32[512]{0:T(512)}, u32[]{:S(2)}) copy-start(f32[512]{0:T(512)} %param.22) | copy-start | bytes 6148
  2.3 19.9 %copy-start.8 = (f32[512]{0:T(512)S(1)}, f32[512]{0:T(512)}, u32[]{:S(2)}) copy-start(f32[512]{0:T(512)} %param.23) | copy-start | bytes 6148
  2.4 19.9 %copy-start.9 = (f32[512]{0:T(512)S(1)}, f32[512]{0:T(512)}, u32[]{:S(2)}) copy-start(f32[512]{0:T(512)} %param.24) | copy-start | bytes 6148
  2.4 19.9 %copy-start.10 = (f32[512]{0:T(512)S(1)}, f32[512]{0:T(512)}, u32[]{:S(2)}) copy-start(f32[512]{0:T(512)} %param.28) | copy-start | bytes 6148
  2.4 19.9 %copy-start.11 = (f32[512]{0:T(512)S(1)}, f32[512]{0:T(512)}, u32[]{:S(2)}) copy-start(f32[512]{0:T(512)} %param.29) | copy-start | bytes 6148
  2.4 19.9 %copy-start.12 = (f32[512]{0:T(512)S(1)}, f32[512]{0:T(512)}, u32[]{:S(2)}) copy-start(f32[512]{0:T(512)} %param.30) | copy-start | bytes 6148
  2.4 20.5 %copy-start.4 = (bf16[256,512]{1,0:T(8,128)(2,1)S(1)}, bf16[256,512]{1,0:T(8,128)(2,1)}, u32[]{:S(2)}) copy-start(bf16[256,512]{1,0:T(8,128)(2,1)} %param.27) | copy-start | bytes 786436
  2.4 20.5 %copy-start.5 = (bf16[256,512]{1,0:T(8,128)(2,1)S(1)}, bf16[256,512]{1,0:T(8,128)(2,1)}, u32[]{:S(2)}) copy-start(bf16[256,512]{1,0:T(8,128)(2,1)} %param.21) | copy-start | bytes 786436
  2.4 10.8 %collective-permute-start = (bf16[400,256]{1,0:T(8,128)(2,1)S(1)}, bf16[400,256]{1,0:T(8,128)(2,1)S(1)}, u32[]{:S(2)}, u32[]{:S(2)}) collective-permute-start(bf16[400,256]{1,0:T(8,128)(2,1)S(1)} %fusion.7), channel_id=1, source_target_pairs={{0,1},{1,0},{2,3},{3,2},{4,5},{5,4},{6,7},{7,6},{8,9},{9,8},{10,11... | collective-permute-start | bytes 614408 | tf_op jit(solution)/shard_map/ppermute | solution.py:816
  5.5 27.8 %collective-permute-start.3 = (bf16[1024,512]{1,0:T(8,128)(2,1)}, bf16[1024,512]{1,0:T(8,128)(2,1)S(1)}, u32[]{:S(2)}, u32[]{:S(2)}) collective-permute-start(bf16[1024,512]{1,0:T(8,128)(2,1)} %refs_12_.1), channel_id=1, source_target_pairs={{0,1},{1,0},{2,3},{3,2},{4,5},{5,4},{6,7},{7,6},{8,9},{9,8},{10,11... | collective-permute-start | bytes 3145736 | tf_op jit(solution)/shard_map/ppermute | solution.py:816
  13.2 6.4 %collective-permute-start.1 = (bf16[384,256]{1,0:T(8,128)(2,1)S(1)}, bf16[384,256]{1,0:T(8,128)(2,1)S(1)}, u32[]{:S(2)}, u32[]{:S(2)}) collective-permute-start(bf16[384,256]{1,0:T(8,128)(2,1)S(1)} %slice.209), channel_id=1, source_target_pairs={{0,4},{2,6},{4,0},{6,2},{8,12},{10,14},{12,8},{14,10},{16,20},{18,... | collective-permute-start | bytes 589832 | tf_op jit(solution)/shard_map/ppermute | solution.py:819
  15.3 7.7 %copy-start.7 = (bf16[2,256]{1,0:T(2,128)(2,1)S(1)}, bf16[2,256]{1,0:T(2,128)(2,1)}, u32[]{:S(2)}) copy-start(bf16[2,256]{1,0:T(2,128)(2,1)} %param.20) | copy-start | bytes 3076
  19.7 4.0 %collective-permute-start.2 = (bf16[768,256]{1,0:T(8,128)(2,1)S(1)}, bf16[768,256]{1,0:T(8,128)(2,1)S(1)}, u32[]{:S(2)}, u32[]{:S(2)}) collective-permute-start(bf16[768,256]{1,0:T(8,128)(2,1)S(1)} %pad_maximum_fusion.4), channel_id=1, source_target_pairs={{0,2},{2,0},{4,6},{6,4},{8,10},{10,8},{12,14},{14,12},{16,18},{18,... | collective-permute-start | bytes 1179656 | tf_op jit(solution)/shard_map/ppermute | solution.py:819
  23.0 10.3 %copy-start.3 = (bf16[784,512]{1,0:T(8,128)(2,1)}, bf16[784,512]{1,0:T(8,128)(2,1)S(1)}, u32[]{:S(2)}) copy-start(bf16[784,512]{1,0:T(8,128)(2,1)S(1)} %fusion.1.w_own_ref) | copy-start | bytes 2408452
  33.3 1.8 %copy-start.13 = (bf16[1024,512]{1,0:T(8,128)(2,1)}, bf16[1024,512]{1,0:T(8,128)(2,1)S(1)}, u32[]{:S(2)}) copy-start(bf16[1024,512]{1,0:T(8,128)(2,1)S(1)} %collective-permute-done.3.x_ref) | copy-start | bytes 3145732
  33.3 24.8 %collective-permute-start.4 = (bf16[784,512]{1,0:T(8,128)(2,1)S(1)}, bf16[784,512]{1,0:T(8,128)(2,1)S(1)}, u32[]{:S(2)}, u32[]{:S(2)}) collective-permute-start(bf16[784,512]{1,0:T(8,128)(2,1)S(1)} %fusion.1.w_own_ref), channel_id=1, source_target_pairs={{0,1},{1,0},{2,3},{3,2},{4,5},{5,4},{6,7},{7,6},{8,9},{9,8},{10,11... | collective-permute-start | bytes 2408456 | tf_op jit(solution)/shard_map/ppermute | solution.py:816
  58.1 0.9 copy-start.14
  72.7 24.8 %collective-permute-start.5 = (bf16[768,512]{1,0:T(8,128)(2,1)}, bf16[768,512]{1,0:T(8,128)(2,1)S(1)}, u32[]{:S(2)}, u32[]{:S(2)}) collective-permute-start(bf16[768,512]{1,0:T(8,128)(2,1)} %get-tuple-element.63), channel_id=1, source_target_pairs={{0,1},{1,0},{2,3},{3,2},{4,5},{5,4},{6,7},{7,6},{8,9},{9,8},{10,11... | collective-permute-start | bytes 2359304 | tf_op jit(solution)/shard_map/ppermute | solution.py:816
  73.6 23.9 %copy-start = (f32[768,512]{1,0:T(8,128)S(1)}, f32[768,512]{1,0:T(8,128)}, u32[]{:S(2)}) copy-start(f32[768,512]{1,0:T(8,128)} %get-tuple-element.62) | copy-start | bytes 4718596
  96.2 25.5 %collective-permute-start.7 = (bf16[1024,512]{1,0:T(8,128)(2,1)}, bf16[1024,512]{1,0:T(8,128)(2,1)S(1)}, u32[]{:S(2)}, u32[]{:S(2)}) collective-permute-start(bf16[1024,512]{1,0:T(8,128)(2,1)} %get-tuple-element.73), channel_id=1, source_target_pairs={{0,1},{1,0},{2,3},{3,2},{4,5},{5,4},{6,7},{7,6},{8,9},{9,8},{10,11... | collective-permute-start | bytes 3145736 | tf_op jit(solution)/shard_map/ppermute | solution.py:816
  97.8 24.0 %collective-permute-start.6 = (bf16[384,512]{1,0:T(8,128)(2,1)S(1)}, bf16[384,512]{1,0:T(8,128)(2,1)}, u32[]{:S(2)}, u32[]{:S(2)}) collective-permute-start(bf16[384,512]{1,0:T(8,128)(2,1)S(1)} %fusion.3), channel_id=1, source_target_pairs={{0,4},{2,6},{4,0},{6,2},{8,12},{10,14},{12,8},{14,10},{16,20},{18,... | collective-permute-start | bytes 1179656 | tf_op jit(solution)/shard_map/ppermute | solution.py:819
  121.8 6.0 %copy-start.1 = (bf16[1024,512]{1,0:T(8,128)(2,1)}, bf16[1024,512]{1,0:T(8,128)(2,1)S(1)}, u32[]{:S(2)}) copy-start(bf16[1024,512]{1,0:T(8,128)(2,1)S(1)} %collective-permute-done.7.got_ref) | copy-start | bytes 3145732
  121.8 4.7 %collective-permute-start.8 = (bf16[1600,256]{1,0:T(8,128)(2,1)}, bf16[1600,256]{1,0:T(8,128)(2,1)}, u32[]{:S(2)}, u32[]{:S(2)}) collective-permute-start(bf16[1600,256]{1,0:T(8,128)(2,1)} %get-tuple-element.82), channel_id=1, source_target_pairs={{0,2},{2,0},{4,6},{6,4},{8,10},{10,8},{12,14},{14,12},{16,18},{18,... | collective-permute-start | bytes 2457608 | tf_op jit(solution)/shard_map/ppermute | solution.py:737
  123.2 3.3 %copy-start.2 = (bf16[1600,256]{1,0:T(8,128)(2,1)S(1)}, bf16[1600,256]{1,0:T(8,128)(2,1)}, u32[]{:S(2)}) copy-start(bf16[1600,256]{1,0:T(8,128)(2,1)} %get-tuple-element.86) | copy-start | bytes 2457604
  123.3 1.5 collective-permute-start.15
  124.8 7.1 %collective-permute-start.16 = (bf16[192,512]{1,0:T(8,128)(2,1)S(1)}, bf16[192,512]{1,0:T(8,128)(2,1)S(1)}, u32[]{:S(2)}, u32[]{:S(2)}) collective-permute-start(bf16[192,512]{1,0:T(8,128)(2,1)S(1)} %fusion.4), channel_id=1, source_target_pairs={{0,8},{2,10},{4,12},{6,14},{8,0},{10,2},{12,4},{14,6},{16,24},{18,... | collective-permute-start | bytes 589832 | tf_op jit(solution)/shard_map/ppermute | solution.py:737
  128.6 11.3 %collective-permute-start.9 = (bf16[800,256]{1,0:T(8,128)(2,1)S(1)}, bf16[800,256]{1,0:T(8,128)(2,1)S(1)}, u32[]{:S(2)}, u32[]{:S(2)}) collective-permute-start(bf16[800,256]{1,0:T(8,128)(2,1)S(1)} %pad_maximum_fusion.3), channel_id=1, source_target_pairs={{0,1},{1,0},{2,3},{3,2},{4,5},{5,4},{6,7},{7,6},{8,9},{9,8},{10,11... | collective-permute-start | bytes 1228808 | tf_op jit(solution)/shard_map/ppermute | solution.py:751
  131.9 11.3 %collective-permute-start.17 = (bf16[192,512]{1,0:T(8,128)(2,1)S(1)}, bf16[192,512]{1,0:T(8,128)(2,1)S(1)}, u32[]{:S(2)}, u32[]{:S(2)}) collective-permute-start(bf16[192,512]{1,0:T(8,128)(2,1)S(1)} %add_convert_fusion.1), channel_id=1, source_target_pairs={{0,16},{2,18},{4,20},{6,22},{8,24},{10,26},{12,28},{14,30},{16,0},... | collective-permute-start | bytes 589832 | tf_op jit(solution)/shard_map/ppermute | solution.py:737
  140.8 6.3 %collective-permute-start.10 = (bf16[416,256]{1,0:T(8,128)(2,1)S(1)}, bf16[416,256]{1,0:T(8,128)(2,1)S(1)}, u32[]{:S(2)}, u32[]{:S(2)}) collective-permute-start(bf16[416,256]{1,0:T(8,128)(2,1)S(1)} %pad_maximum_fusion.8), channel_id=1, source_target_pairs={{0,4},{2,6},{4,0},{6,2},{8,12},{10,14},{12,8},{14,10},{16,20},{18,... | collective-permute-start | bytes 638984 | tf_op jit(solution)/shard_map/ppermute | solution.py:737
  143.3 4.4 %collective-permute-start.18 = (bf16[192,512]{1,0:T(8,128)(2,1)S(1)}, bf16[192,512]{1,0:T(8,128)(2,1)S(1)}, u32[]{:S(2)}, u32[]{:S(2)}) collective-permute-start(bf16[192,512]{1,0:T(8,128)(2,1)S(1)} %add_convert_fusion), channel_id=1, source_target_pairs={{0,2},{2,0},{4,6},{6,4},{8,10},{10,8},{12,14},{14,12},{16,18},{18,... | collective-permute-start | bytes 589832 | tf_op jit(solution)/shard_map/ppermute | solution.py:737
  147.2 5.9 %collective-permute-start.11 = (bf16[416,256]{1,0:T(8,128)(2,1)S(1)}, bf16[416,256]{1,0:T(8,128)(2,1)S(1)}, u32[]{:S(2)}, u32[]{:S(2)}) collective-permute-start(bf16[416,256]{1,0:T(8,128)(2,1)S(1)} %pad_maximum_fusion.9), channel_id=1, source_target_pairs={{0,8},{2,10},{4,12},{6,14},{8,0},{10,2},{12,4},{14,6},{16,24},{18,... | collective-permute-start | bytes 638984 | tf_op jit(solution)/shard_map/ppermute | solution.py:737
  147.8 17.0 %collective-permute-start.19 = (bf16[384,512]{1,0:T(8,128)(2,1)S(1)}, bf16[384,512]{1,0:T(8,128)(2,1)S(1)}, u32[]{:S(2)}, u32[]{:S(2)}) collective-permute-start(bf16[384,512]{1,0:T(8,128)(2,1)S(1)} %pad_maximum_fusion.6), channel_id=1, source_target_pairs={{0,4},{2,6},{4,0},{6,2},{8,12},{10,14},{12,8},{14,10},{16,20},{18,... | collective-permute-start | bytes 1179656 | tf_op jit(solution)/shard_map/ppermute | solution.py:737
  153.2 11.5 %collective-permute-start.12 = (bf16[416,256]{1,0:T(8,128)(2,1)S(1)}, bf16[416,256]{1,0:T(8,128)(2,1)S(1)}, u32[]{:S(2)}, u32[]{:S(2)}) collective-permute-start(bf16[416,256]{1,0:T(8,128)(2,1)S(1)} %pad_maximum_fusion.10), channel_id=1, source_target_pairs={{0,16},{2,18},{4,20},{6,22},{8,24},{10,26},{12,28},{14,30},{16,0},... | collective-permute-start | bytes 638984 | tf_op jit(solution)/shard_map/ppermute | solution.py:737
  164.8 5.7 %collective-permute-start.13 = (bf16[384,256]{1,0:T(8,128)(2,1)S(1)}, bf16[384,256]{1,0:T(8,128)(2,1)S(1)}, u32[]{:S(2)}, u32[]{:S(2)}) collective-permute-start(bf16[384,256]{1,0:T(8,128)(2,1)S(1)} %add_convert_fusion.2), channel_id=1, source_target_pairs={{0,4},{2,6},{4,0},{6,2},{8,12},{10,14},{12,8},{14,10},{16,20},{18,... | collective-permute-start | bytes 589832 | tf_op jit(solution)/shard_map/ppermute | solution.py:737
  170.6 1.8 %collective-permute-start.14 = (bf16[768,256]{1,0:T(8,128)(2,1)S(1)}, bf16[768,256]{1,0:T(8,128)(2,1)S(1)}, u32[]{:S(2)}, u32[]{:S(2)}) collective-permute-start(bf16[768,256]{1,0:T(8,128)(2,1)S(1)} %pad_maximum_fusion.5), channel_id=1, source_target_pairs={{0,2},{2,0},{4,6},{6,4},{8,10},{10,8},{12,14},{14,12},{16,18},{18,... | collective-permute-start | bytes 1179656 | tf_op jit(solution)/shard_map/ppermute | solution.py:737

commit v3 on v2

--- a/solution.py
+++ b/solution.py
@@ -516,7 +516,7 @@
         copy.start()
 
     def work(size, rolled):
-        block, rows = size // 2, size // 4
+        block, rows = size // 2, size // 2
         low = lax.broadcasted_iota(jnp.int32, (rows, LANES), 1) < HD
         if size < keys:
             dk_ref[size:, :] = jnp.zeros((keys - size, width), BF)
@@ -567,7 +567,7 @@
                     return tuple(total)
 
                 zero = jnp.zeros((LANES, queries), F32)
-                for side, total in enumerate(sweep(rolled, block, 2, at_rows, (zero, zero))):
+                for side, total in enumerate(sweep(rolled, block, 1, at_rows, (zero, zero))):
                     acc_scr[side] += total
 
             pl.loop(0, 2)(one_block)

time: 175 us -> 174 us (level)
  no operation moved by 1% of the time
where the time goes in v3:
time: 174 us
  Pallas kernels  96.7 us (56%)
  starting transfers between devices  25.6 us (15%)
  waiting for transfers between devices  24.4 us (14%)
  other arithmetic  19.6 us (11%)
  local copies, waits for them, and re-layouts  6.22 us (4%)
    pallas_call x2, Pallas kernels, attend_backward(): pl.pallas_call(functools.partial(backward_kernel, sub, part), out_shape=o...  44.2 us
    pallas_call x1, Pallas kernels, attend(): pl.pallas_call(functools.partial(attend_kernel, count, chunk), out_shape=...  23.1 us
    ppermute x14, waiting for transfers between devices, across(): return lax.ppermute(values, 'dp', [(i, i ^ bit) for i in range(devices)])  18.4 us
    ppermute x14, starting transfers between devices, across(): return lax.ppermute(values, 'dp', [(i, i ^ bit) for i in range(devices)])  17.7 us
    pallas_call x1, Pallas kernels, middle(): pl.pallas_call(functools.partial(middle_kernel, sub), grid=(tokens // blo...  13.6 us
    pallas_call x1, Pallas kernels, project(): pl.pallas_call(project_kernel, grid=(tokens // block,), out_shape=(jax.Sh...  8.41 us
    pallas_call x1, Pallas kernels, input_gradient(): pl.pallas_call(input_kernel, grid=(tokens // 256,), out_shape=jax.ShapeDt...  7.34 us
    ppermute x5, starting transfers between devices, swapped(): return lax.ppermute(values, 'tensor', [(0, 1), (1, 0)])  7.01 us
  transfers between devices with their start and end apart: 20, of which 10 were waited for; matrix products, arithmetic and copies ran while one was open for 12% of the time, Pallas kernels for 48%

profile of v3, /device:TPU:0, one launch (start us, length us, event | category | flops | bytes accessed | tf_op | source)
XLA Modules:
  0.0 173.7 jit_solution(2664630757239828688)
XLA Ops:
  0.7 0.9 constant_dynamic-slice_fusion.4
  1.6 0.7 fusion.7
  2.4 3.0 %collective-permute-start = (bf16[400,256]{1,0:T(8,128)(2,1)S(1)}, bf16[400,256]{1,0:T(8,128)(2,1)S(1)}, u32[]{:S(2)}, u32[]{:S(2)}) collective-permute-start(bf16[400,256]{1,0:T(8,128)(2,1)S(1)} %fusion.7), channel_id=1, source_target_pairs={{0,1},{1,0},{2,3},{3,2},{4,5},{5,4},{6,7},{7,6},{8,9},{9,8},{10,11... | collective-permute-start | bytes 614408 | tf_op jit(solution)/shard_map/ppermute | solution.py:816
  5.5 0.7 compare_bitcast_fusion
  6.2 0.8 reduce-window.10
  7.0 0.7 fusion.29
  7.7 0.7 bitcast_subtract_fusion
  8.5 0.7 broadcast_compare_fusion
  10.9 0.7 fusion.10.extra_q_ref
  12.2 1.0 fusion.34
  13.2 2.0 %collective-permute-start.1 = (bf16[384,256]{1,0:T(8,128)(2,1)S(1)}, bf16[384,256]{1,0:T(8,128)(2,1)S(1)}, u32[]{:S(2)}, u32[]{:S(2)}) collective-permute-start(bf16[384,256]{1,0:T(8,128)(2,1)S(1)} %slice.209), channel_id=1, source_target_pairs={{0,4},{2,6},{4,0},{6,2},{8,12},{10,14},{12,8},{14,10},{16,20},{18,... | collective-permute-start | bytes 589832 | tf_op jit(solution)/shard_map/ppermute | solution.py:819
  15.3 4.4 %collective-permute-done.1 = bf16[384,256]{1,0:T(8,128)(2,1)S(1)} collective-permute-done((bf16[384,256]{1,0:T(8,128)(2,1)S(1)}, bf16[384,256]{1,0:T(8,128)(2,1)S(1)}, u32[]{:S(2)}, u32[]{:S(2)}) %collective-permute-start.1) | collective-permute-done | bytes 196640 | tf_op jit(solution)/shard_map/ppermute | solution.py:819
  21.0 1.2 pad_add_fusion.live_ref.refs_0_
  23.0 0.7 maximum_convert_fusion.bias_ref
  23.9 1.0 pad_maximum_fusion
  24.8 8.4 %project.1 = (bf16[8,1024,128]{2,1,0:T(8,128)(2,1)}, bf16[8,1024,128]{2,1,0:T(8,128)(2,1)}, bf16[1024,512]{1,0:T(8,128)(2,1)}, bf16[8,128,1024]{2,1,0:T(8,128)(2,1)}, bf16[1024,512]{1,0:T(8,128)(2,1)}) custom-call(bf16[1024,512]{1,0:T(8,128)(2,1)} %refs_12_.1, bf16[3,512,256]{2,1,0:T(8,128)(2,1)} %bitcast.89, bf16[3,512,256]{2,1,0:T(8,128)(2,1)} %bitcast.79, ...), custom_call_target="tpu_custom_call" | custom-call | flops 2684354560 | bytes 6291456 | tf_op jit(solution)/shard_map/project/pallas_call | solution.py:96
  33.3 1.7 %collective-permute-start.4 = (bf16[784,512]{1,0:T(8,128)(2,1)S(1)}, bf16[784,512]{1,0:T(8,128)(2,1)S(1)}, u32[]{:S(2)}, u32[]{:S(2)}) collective-permute-start(bf16[784,512]{1,0:T(8,128)(2,1)S(1)} %fusion.1.w_own_ref), channel_id=1, source_target_pairs={{0,1},{1,0},{2,3},{3,2},{4,5},{5,4},{6,7},{7,6},{8,9},{9,8},{10,11... | collective-permute-start | bytes 2408456 | tf_op jit(solution)/shard_map/ppermute | solution.py:816
  35.0 23.1 %attend.1 = (bf16[8,2048,1024]{2,1,0:T(8,128)(2,1)}, f32[8,64,1024]{2,1,0:T(8,128)}, f32[8,1,1024]{2,1,0:T(1,128)}, bf16[8,1024,128]{2,1,0:T(8,128)(2,1)}, bf16[...) custom-call(s32[2]{0:T(128)} %pad_add_fusion.live_ref.refs_0_, bf16[8,128,1024]{2,1,0:T(8,128)(2,1)} %get-tuple-element.52.qt_hbm, ...), custom_call_target="tpu_custom_call" | custom-call | flops 17179869184 | bytes 33554432 | tf_op jit(solution)/shard_map/attend/pallas_call | solution.py:282
  58.1 0.9 copy-done.14
  59.0 13.6 %middle.1 = (bf16[1024,512]{1,0:T(8,128)(2,1)}, f32[1024,512]{1,0:T(8,128)}, bf16[8,128,1024]{2,1,0:T(8,128)(2,1)}, bf16[1024,512]{1,0:T(8,128)(2,1)}, f32[768,5...) custom-call(bf16[1024,512]{1,0:T(8,128)(2,1)} %refs_12_.1, bf16[1024,512]{1,0:T(8,128)(2,1)} %cot_ref.1, ...), custom_call_target="tpu_custom_call" | custom-call | flops 4831838208 | bytes 10485760 | tf_op jit(solution)/shard_map/middle/pallas_call | solution.py:433
  72.7 0.9 collective-permute-start.5
  73.6 22.5 %attend_back_other.1 = (f32[512,1024]{1,0:T(8,128)}, bf16[1024,512]{1,0:T(8,128)(2,1)}, f32[2,512,512]{2,1,0:T(8,128)}, f32[2,512]{1,0:T(2,128)}) custom-call(s32[2]{0:T(128)} %pad_add_fusion.live_ref.refs_0_, bf16[8,2048,1024]{2,1,0:T(8,128)(2,1)} %get-tuple-element.64.refs_1_.refs_3_, bf16[8,128,1024]{2,1,0:T(8,128)(2,1)} %get-tuple-element.65.refs_2_.refs_4_, ...), custom_call_target="tpu_custom_call" | custom-call | flops 17179869184 | bytes 16777216 | tf_op jit(solution)/shard_map/attend_back_other/pallas_call | solution.py:655
  96.1 1.2 collective-permute-start.7
  97.6 1.5 collective-permute-start.6
  99.2 21.8 %attend_back_own.1 = (bf16[1600,256]{1,0:T(8,128)(2,1)}, bf16[1600,256]{1,0:T(8,128)(2,1)}, bf16[1024,512]{1,0:T(8,128)(2,1)}, bf16[1024,512]{1,0:T(8,128)(2,1)}, bf16[1024,512]{1,0:T(8,128)(2,1)}) custom-call(s32[2]{0:T(128)} %pad_add_fusion.live_ref.refs_0_, f32[8,512]{1,0:T(8,128)} %get-tuple-element.74.refs_1_, f32[2,512]{1,0:T(2,128)} %get-tuple-element.75.refs_2_, ...), custom_call_target="tpu_custom_call" | custom-call | flops 17179869184 | bytes 16777216 | tf_op jit(solution)/shard_map/attend_back_own/pallas_call | solution.py:655
  120.9 0.7 collective-permute-done.7.got_ref
  121.6 1.4 bitcast_add_fusion
  123.4 1.3 collective-permute-done.15
  124.7 1.6 collective-permute-start.16
  126.3 1.3 convert_add_fusion
  127.7 0.7 subtract_convert_fusion
  128.4 0.9 collective-permute-start.9
  129.4 2.4 %collective-permute-done.16 = bf16[192,512]{1,0:T(8,128)(2,1)S(1)} collective-permute-done((bf16[192,512]{1,0:T(8,128)(2,1)S(1)}, bf16[192,512]{1,0:T(8,128)(2,1)S(1)}, u32[]{:S(2)}, u32[]{:S(2)}) %collective-permute-start.16) | collective-permute-done | bytes 196640 | tf_op jit(solution)/shard_map/ppermute | solution.py:737
  131.8 2.7 %collective-permute-start.17 = (bf16[192,512]{1,0:T(8,128)(2,1)S(1)}, bf16[192,512]{1,0:T(8,128)(2,1)S(1)}, u32[]{:S(2)}, u32[]{:S(2)}) collective-permute-start(bf16[192,512]{1,0:T(8,128)(2,1)S(1)} %add_convert_fusion.1), channel_id=1, source_target_pairs={{0,16},{2,18},{4,20},{6,22},{8,24},{10,26},{12,28},{14,30},{16,0},... | collective-permute-start | bytes 589832 | tf_op jit(solution)/shard_map/ppermute | solution.py:737
  134.4 5.3 %collective-permute-done.9 = bf16[800,256]{1,0:T(8,128)(2,1)S(1)} collective-permute-done((bf16[800,256]{1,0:T(8,128)(2,1)S(1)}, bf16[800,256]{1,0:T(8,128)(2,1)S(1)}, u32[]{:S(2)}, u32[]{:S(2)}) %collective-permute-start.9) | collective-permute-done | bytes 409632 | tf_op jit(solution)/shard_map/ppermute | solution.py:751
  139.9 0.7 fusion.16
  140.7 1.6 collective-permute-start.10
  142.2 0.9 collective-permute-done.17
  143.3 3.7 %collective-permute-done.10 = bf16[416,256]{1,0:T(8,128)(2,1)S(1)} collective-permute-done((bf16[416,256]{1,0:T(8,128)(2,1)S(1)}, bf16[416,256]{1,0:T(8,128)(2,1)S(1)}, u32[]{:S(2)}, u32[]{:S(2)}) %collective-permute-start.10) | collective-permute-done | bytes 213024 | tf_op jit(solution)/shard_map/ppermute | solution.py:737
  147.6 1.6 collective-permute-start.19
  149.2 3.7 %collective-permute-done.11 = bf16[416,256]{1,0:T(8,128)(2,1)S(1)} collective-permute-done((bf16[416,256]{1,0:T(8,128)(2,1)S(1)}, bf16[416,256]{1,0:T(8,128)(2,1)S(1)}, u32[]{:S(2)}, u32[]{:S(2)}) %collective-permute-start.11) | collective-permute-done | bytes 213024 | tf_op jit(solution)/shard_map/ppermute | solution.py:737
  153.0 4.2 %collective-permute-start.12 = (bf16[416,256]{1,0:T(8,128)(2,1)S(1)}, bf16[416,256]{1,0:T(8,128)(2,1)S(1)}, u32[]{:S(2)}, u32[]{:S(2)}) collective-permute-start(bf16[416,256]{1,0:T(8,128)(2,1)S(1)} %pad_maximum_fusion.10), channel_id=1, source_target_pairs={{0,16},{2,18},{4,20},{6,22},{8,24},{10,26},{12,28},{14,30},{16,0},... | collective-permute-start | bytes 638984 | tf_op jit(solution)/shard_map/ppermute | solution.py:737
  157.2 7.3 %input_gradient.1 = f32[1024,512]{1,0:T(8,128)} custom-call(f32[1024,512]{1,0:T(8,128)} %get-tuple-element.61.res_ref, bf16[1024,512]{1,0:T(8,128)(2,1)} %copy-done.1, bf16[1024,512]{1,0:T(8,128)(2,1)} %get-tuple-element.83.dq_ref, bf16[1024,512]{1,0:T(8,128)(2,1)} %get-tuple-element.84.dk_ref, bf16[1024,512]{1,0:T(8,128)(2,1)} %get-tuple-element.85.dv_ref, ...), custom_call_target="tpu_custom_call" | custom-call | flops 1610612736 | bytes 8388608 | tf_op jit(solution)/shard_map/input_gradient/pallas_call | solution.py:696
  164.7 1.5 collective-permute-start.13
  166.3 1.2 fusion.6
  168.6 1.8 %collective-permute-done.13 = bf16[384,256]{1,0:T(8,128)(2,1)S(1)} collective-permute-done((bf16[384,256]{1,0:T(8,128)(2,1)S(1)}, bf16[384,256]{1,0:T(8,128)(2,1)S(1)}, u32[]{:S(2)}, u32[]{:S(2)}) %collective-permute-start.13) | collective-permute-done | bytes 196640 | tf_op jit(solution)/shard_map/ppermute | solution.py:737
  171.2 0.8 pad_maximum_fusion.2
  172.5 1.3 convert_bitcast_fusion
  (113 shorter events, 9.2 us)
Async XLA Ops:
  2.3 19.9 %copy-start.15 = (bf16[256]{0:T(256)(128)(2,1)S(1)}, bf16[256]{0:T(256)(128)(2,1)}, u32[]{:S(2)}) copy-start(bf16[256]{0:T(256)(128)(2,1)} %param.26) | copy-start | bytes 1540
  2.3 19.9 %copy-start.6 = (f32[512]{0:T(512)S(1)}, f32[512]{0:T(512)}, u32[]{:S(2)}) copy-start(f32[512]{0:T(512)} %param.22) | copy-start | bytes 6148
  2.3 19.9 %copy-start.8 = (f32[512]{0:T(512)S(1)}, f32[512]{0:T(512)}, u32[]{:S(2)}) copy-start(f32[512]{0:T(512)} %param.23) | copy-start | bytes 6148
  2.4 19.9 %copy-start.9 = (f32[512]{0:T(512)S(1)}, f32[512]{0:T(512)}, u32[]{:S(2)}) copy-start(f32[512]{0:T(512)} %param.24) | copy-start | bytes 6148
  2.4 19.9 %copy-start.10 = (f32[512]{0:T(512)S(1)}, f32[512]{0:T(512)}, u32[]{:S(2)}) copy-start(f32[512]{0:T(512)} %param.28) | copy-start | bytes 6148
  2.4 19.9 %copy-start.11 = (f32[512]{0:T(512)S(1)}, f32[512]{0:T(512)}, u32[]{:S(2)}) copy-start(f32[512]{0:T(512)} %param.29) | copy-start | bytes 6148
  2.4 19.9 %copy-start.12 = (f32[512]{0:T(512)S(1)}, f32[512]{0:T(512)}, u32[]{:S(2)}) copy-start(f32[512]{0:T(512)} %param.30) | copy-start | bytes 6148
  2.4 20.5 %copy-start.4 = (bf16[256,512]{1,0:T(8,128)(2,1)S(1)}, bf16[256,512]{1,0:T(8,128)(2,1)}, u32[]{:S(2)}) copy-start(bf16[256,512]{1,0:T(8,128)(2,1)} %param.27) | copy-start | bytes 786436
  2.4 20.5 %copy-start.5 = (bf16[256,512]{1,0:T(8,128)(2,1)S(1)}, bf16[256,512]{1,0:T(8,128)(2,1)}, u32[]{:S(2)}) copy-start(bf16[256,512]{1,0:T(8,128)(2,1)} %param.21) | copy-start | bytes 786436
  2.4 10.8 %collective-permute-start = (bf16[400,256]{1,0:T(8,128)(2,1)S(1)}, bf16[400,256]{1,0:T(8,128)(2,1)S(1)}, u32[]{:S(2)}, u32[]{:S(2)}) collective-permute-start(bf16[400,256]{1,0:T(8,128)(2,1)S(1)} %fusion.7), channel_id=1, source_target_pairs={{0,1},{1,0},{2,3},{3,2},{4,5},{5,4},{6,7},{7,6},{8,9},{9,8},{10,11... | collective-permute-start | bytes 614408 | tf_op jit(solution)/shard_map/ppermute | solution.py:816
  5.5 27.8 %collective-permute-start.3 = (bf16[1024,512]{1,0:T(8,128)(2,1)}, bf16[1024,512]{1,0:T(8,128)(2,1)S(1)}, u32[]{:S(2)}, u32[]{:S(2)}) collective-permute-start(bf16[1024,512]{1,0:T(8,128)(2,1)} %refs_12_.1), channel_id=1, source_target_pairs={{0,1},{1,0},{2,3},{3,2},{4,5},{5,4},{6,7},{7,6},{8,9},{9,8},{10,11... | collective-permute-start | bytes 3145736 | tf_op jit(solution)/shard_map/ppermute | solution.py:816
  13.2 6.4 %collective-permute-start.1 = (bf16[384,256]{1,0:T(8,128)(2,1)S(1)}, bf16[384,256]{1,0:T(8,128)(2,1)S(1)}, u32[]{:S(2)}, u32[]{:S(2)}) collective-permute-start(bf16[384,256]{1,0:T(8,128)(2,1)S(1)} %slice.209), channel_id=1, source_target_pairs={{0,4},{2,6},{4,0},{6,2},{8,12},{10,14},{12,8},{14,10},{16,20},{18,... | collective-permute-start | bytes 589832 | tf_op jit(solution)/shard_map/ppermute | solution.py:819
  15.3 7.7 %copy-start.7 = (bf16[2,256]{1,0:T(2,128)(2,1)S(1)}, bf16[2,256]{1,0:T(2,128)(2,1)}, u32[]{:S(2)}) copy-start(bf16[2,256]{1,0:T(2,128)(2,1)} %param.20) | copy-start | bytes 3076
  19.7 4.0 %collective-permute-start.2 = (bf16[768,256]{1,0:T(8,128)(2,1)S(1)}, bf16[768,256]{1,0:T(8,128)(2,1)S(1)}, u32[]{:S(2)}, u32[]{:S(2)}) collective-permute-start(bf16[768,256]{1,0:T(8,128)(2,1)S(1)} %pad_maximum_fusion.4), channel_id=1, source_target_pairs={{0,2},{2,0},{4,6},{6,4},{8,10},{10,8},{12,14},{14,12},{16,18},{18,... | collective-permute-start | bytes 1179656 | tf_op jit(solution)/shard_map/ppermute | solution.py:819
  23.0 10.3 %copy-start.3 = (bf16[784,512]{1,0:T(8,128)(2,1)}, bf16[784,512]{1,0:T(8,128)(2,1)S(1)}, u32[]{:S(2)}) copy-start(bf16[784,512]{1,0:T(8,128)(2,1)S(1)} %fusion.1.w_own_ref) | copy-start | bytes 2408452
  33.3 1.8 %copy-start.13 = (bf16[1024,512]{1,0:T(8,128)(2,1)}, bf16[1024,512]{1,0:T(8,128)(2,1)S(1)}, u32[]{:S(2)}) copy-start(bf16[1024,512]{1,0:T(8,128)(2,1)S(1)} %collective-permute-done.3.x_ref) | copy-start | bytes 3145732
  33.3 24.8 %collective-permute-start.4 = (bf16[784,512]{1,0:T(8,128)(2,1)S(1)}, bf16[784,512]{1,0:T(8,128)(2,1)S(1)}, u32[]{:S(2)}, u32[]{:S(2)}) collective-permute-start(bf16[784,512]{1,0:T(8,128)(2,1)S(1)} %fusion.1.w_own_ref), channel_id=1, source_target_pairs={{0,1},{1,0},{2,3},{3,2},{4,5},{5,4},{6,7},{7,6},{8,9},{9,8},{10,11... | collective-permute-start | bytes 2408456 | tf_op jit(solution)/shard_map/ppermute | solution.py:816
  58.1 0.9 copy-start.14
  72.7 24.6 %collective-permute-start.5 = (bf16[768,512]{1,0:T(8,128)(2,1)}, bf16[768,512]{1,0:T(8,128)(2,1)S(1)}, u32[]{:S(2)}, u32[]{:S(2)}) collective-permute-start(bf16[768,512]{1,0:T(8,128)(2,1)} %get-tuple-element.63), channel_id=1, source_target_pairs={{0,1},{1,0},{2,3},{3,2},{4,5},{5,4},{6,7},{7,6},{8,9},{9,8},{10,11... | collective-permute-start | bytes 2359304 | tf_op jit(solution)/shard_map/ppermute | solution.py:816
  73.6 23.7 %copy-start = (f32[768,512]{1,0:T(8,128)S(1)}, f32[768,512]{1,0:T(8,128)}, u32[]{:S(2)}) copy-start(f32[768,512]{1,0:T(8,128)} %get-tuple-element.62) | copy-start | bytes 4718596
  96.1 25.5 %collective-permute-start.7 = (bf16[1024,512]{1,0:T(8,128)(2,1)}, bf16[1024,512]{1,0:T(8,128)(2,1)S(1)}, u32[]{:S(2)}, u32[]{:S(2)}) collective-permute-start(bf16[1024,512]{1,0:T(8,128)(2,1)} %get-tuple-element.73), channel_id=1, source_target_pairs={{0,1},{1,0},{2,3},{3,2},{4,5},{5,4},{6,7},{7,6},{8,9},{9,8},{10,11... | collective-permute-start | bytes 3145736 | tf_op jit(solution)/shard_map/ppermute | solution.py:816
  97.6 24.0 %collective-permute-start.6 = (bf16[384,512]{1,0:T(8,128)(2,1)S(1)}, bf16[384,512]{1,0:T(8,128)(2,1)}, u32[]{:S(2)}, u32[]{:S(2)}) collective-permute-start(bf16[384,512]{1,0:T(8,128)(2,1)S(1)} %fusion.3), channel_id=1, source_target_pairs={{0,4},{2,6},{4,0},{6,2},{8,12},{10,14},{12,8},{14,10},{16,20},{18,... | collective-permute-start | bytes 1179656 | tf_op jit(solution)/shard_map/ppermute | solution.py:819
  121.6 6.0 %copy-start.1 = (bf16[1024,512]{1,0:T(8,128)(2,1)}, bf16[1024,512]{1,0:T(8,128)(2,1)S(1)}, u32[]{:S(2)}) copy-start(bf16[1024,512]{1,0:T(8,128)(2,1)S(1)} %collective-permute-done.7.got_ref) | copy-start | bytes 3145732
  121.6 4.7 %collective-permute-start.8 = (bf16[1600,256]{1,0:T(8,128)(2,1)}, bf16[1600,256]{1,0:T(8,128)(2,1)}, u32[]{:S(2)}, u32[]{:S(2)}) collective-permute-start(bf16[1600,256]{1,0:T(8,128)(2,1)} %get-tuple-element.82), channel_id=1, source_target_pairs={{0,2},{2,0},{4,6},{6,4},{8,10},{10,8},{12,14},{14,12},{16,18},{18,... | collective-permute-start | bytes 2457608 | tf_op jit(solution)/shard_map/ppermute | solution.py:737
  123.1 3.3 %copy-start.2 = (bf16[1600,256]{1,0:T(8,128)(2,1)S(1)}, bf16[1600,256]{1,0:T(8,128)(2,1)}, u32[]{:S(2)}) copy-start(bf16[1600,256]{1,0:T(8,128)(2,1)} %get-tuple-element.86) | copy-start | bytes 2457604
  123.1 1.5 collective-permute-start.15
  124.7 7.1 %collective-permute-start.16 = (bf16[192,512]{1,0:T(8,128)(2,1)S(1)}, bf16[192,512]{1,0:T(8,128)(2,1)S(1)}, u32[]{:S(2)}, u32[]{:S(2)}) collective-permute-start(bf16[192,512]{1,0:T(8,128)(2,1)S(1)} %fusion.4), channel_id=1, source_target_pairs={{0,8},{2,10},{4,12},{6,14},{8,0},{10,2},{12,4},{14,6},{16,24},{18,... | collective-permute-start | bytes 589832 | tf_op jit(solution)/shard_map/ppermute | solution.py:737
  128.4 11.3 %collective-permute-start.9 = (bf16[800,256]{1,0:T(8,128)(2,1)S(1)}, bf16[800,256]{1,0:T(8,128)(2,1)S(1)}, u32[]{:S(2)}, u32[]{:S(2)}) collective-permute-start(bf16[800,256]{1,0:T(8,128)(2,1)S(1)} %pad_maximum_fusion.3), channel_id=1, source_target_pairs={{0,1},{1,0},{2,3},{3,2},{4,5},{5,4},{6,7},{7,6},{8,9},{9,8},{10,11... | collective-permute-start | bytes 1228808 | tf_op jit(solution)/shard_map/ppermute | solution.py:751
  131.8 11.3 %collective-permute-start.17 = (bf16[192,512]{1,0:T(8,128)(2,1)S(1)}, bf16[192,512]{1,0:T(8,128)(2,1)S(1)}, u32[]{:S(2)}, u32[]{:S(2)}) collective-permute-start(bf16[192,512]{1,0:T(8,128)(2,1)S(1)} %add_convert_fusion.1), channel_id=1, source_target_pairs={{0,16},{2,18},{4,20},{6,22},{8,24},{10,26},{12,28},{14,30},{16,0},... | collective-permute-start | bytes 589832 | tf_op jit(solution)/shard_map/ppermute | solution.py:737
  140.7 6.3 %collective-permute-start.10 = (bf16[416,256]{1,0:T(8,128)(2,1)S(1)}, bf16[416,256]{1,0:T(8,128)(2,1)S(1)}, u32[]{:S(2)}, u32[]{:S(2)}) collective-permute-start(bf16[416,256]{1,0:T(8,128)(2,1)S(1)} %pad_maximum_fusion.8), channel_id=1, source_target_pairs={{0,4},{2,6},{4,0},{6,2},{8,12},{10,14},{12,8},{14,10},{16,20},{18,... | collective-permute-start | bytes 638984 | tf_op jit(solution)/shard_map/ppermute | solution.py:737
  143.2 4.4 %collective-permute-start.18 = (bf16[192,512]{1,0:T(8,128)(2,1)S(1)}, bf16[192,512]{1,0:T(8,128)(2,1)S(1)}, u32[]{:S(2)}, u32[]{:S(2)}) collective-permute-start(bf16[192,512]{1,0:T(8,128)(2,1)S(1)} %add_convert_fusion), channel_id=1, source_target_pairs={{0,2},{2,0},{4,6},{6,4},{8,10},{10,8},{12,14},{14,12},{16,18},{18,... | collective-permute-start | bytes 589832 | tf_op jit(solution)/shard_map/ppermute | solution.py:737
  147.0 5.9 %collective-permute-start.11 = (bf16[416,256]{1,0:T(8,128)(2,1)S(1)}, bf16[416,256]{1,0:T(8,128)(2,1)S(1)}, u32[]{:S(2)}, u32[]{:S(2)}) collective-permute-start(bf16[416,256]{1,0:T(8,128)(2,1)S(1)} %pad_maximum_fusion.9), channel_id=1, source_target_pairs={{0,8},{2,10},{4,12},{6,14},{8,0},{10,2},{12,4},{14,6},{16,24},{18,... | collective-permute-start | bytes 638984 | tf_op jit(solution)/shard_map/ppermute | solution.py:737
  147.6 17.0 %collective-permute-start.19 = (bf16[384,512]{1,0:T(8,128)(2,1)S(1)}, bf16[384,512]{1,0:T(8,128)(2,1)S(1)}, u32[]{:S(2)}, u32[]{:S(2)}) collective-permute-start(bf16[384,512]{1,0:T(8,128)(2,1)S(1)} %pad_maximum_fusion.6), channel_id=1, source_target_pairs={{0,4},{2,6},{4,0},{6,2},{8,12},{10,14},{12,8},{14,10},{16,20},{18,... | collective-permute-start | bytes 1179656 | tf_op jit(solution)/shard_map/ppermute | solution.py:737
  153.0 11.5 %collective-permute-start.12 = (bf16[416,256]{1,0:T(8,128)(2,1)S(1)}, bf16[416,256]{1,0:T(8,128)(2,1)S(1)}, u32[]{:S(2)}, u32[]{:S(2)}) collective-permute-start(bf16[416,256]{1,0:T(8,128)(2,1)S(1)} %pad_maximum_fusion.10), channel_id=1, source_target_pairs={{0,16},{2,18},{4,20},{6,22},{8,24},{10,26},{12,28},{14,30},{16,0},... | collective-permute-start | bytes 638984 | tf_op jit(solution)/shard_map/ppermute | solution.py:737
  164.7 5.7 %collective-permute-start.13 = (bf16[384,256]{1,0:T(8,128)(2,1)S(1)}, bf16[384,256]{1,0:T(8,128)(2,1)S(1)}, u32[]{:S(2)}, u32[]{:S(2)}) collective-permute-start(bf16[384,256]{1,0:T(8,128)(2,1)S(1)} %add_convert_fusion.2), channel_id=1, source_target_pairs={{0,4},{2,6},{4,0},{6,2},{8,12},{10,14},{12,8},{14,10},{16,20},{18,... | collective-permute-start | bytes 589832 | tf_op jit(solution)/shard_map/ppermute | solution.py:737
  170.5 1.8 %collective-permute-start.14 = (bf16[768,256]{1,0:T(8,128)(2,1)S(1)}, bf16[768,256]{1,0:T(8,128)(2,1)S(1)}, u32[]{:S(2)}, u32[]{:S(2)}) collective-permute-start(bf16[768,256]{1,0:T(8,128)(2,1)S(1)} %pad_maximum_fusion.5), channel_id=1, source_target_pairs={{0,2},{2,0},{4,6},{6,4},{8,10},{10,8},{12,14},{14,12},{16,18},{18,... | collective-permute-start | bytes 1179656 | tf_op jit(solution)/shard_map/ppermute | solution.py:737
